TPU v7x, 128 devices: a whole 4x4x4 slice. The times are simulated.
128 devices in a mesh: ctx: 32 (over y, x, core), exp: 4 (over z).
Axes of the slice: x: 4, y: 4, z: 4, core: 2. Of those that a mesh axis runs over, the one named last changes fastest.
Arguments:
- filter_entry_array: bfloat16 [16384, 2176], P(('ctx', 'exp')), may hold values from -6 to 6
- gate_input: bfloat16 [16384, 2048], P(('ctx', 'exp')), may hold values from -20 to 20
- step_unshifted: float32 [32, 16384], P(None, ('ctx', 'exp')), may hold values from -4 to 16
- step_bias: float32 [32], replicated, may hold values from -11 to -2
- decay_log: float32 [32], replicated, may hold values from -3.2 to -0.2
- conv_weight: float32 [4, 2176], replicated, may hold values from -3 to 3
- conv_bias: float32 [2176], replicated, may hold values from -3 to 3
- skip_gain: float32 [32], replicated, may hold values from 0.5 to 1.5
- mixer_gain: float32 [2048], replicated, may hold values from 0.25 to 1.75
- residual: bfloat16 [16384, 2048], P(('ctx', 'exp')), may hold values from -14 to 14
- expert_norm: float32 [2048], replicated, may hold values from 0.25 to 1.75
- router_weight: bfloat16 [2048, 32], replicated, may hold values from -0.25 to 0.25
- expert_ids: int32 [16384, 8], P(('ctx', 'exp')), may hold values from 0 to 31, all different within a row; in each aligned block of 128 rows (0 to 127, 128 to 255, ...) at most 40 rows name the same one
- w_gate: bfloat16 [32, 2048, 768], P('ctx'), may hold values from -0.125 to 0.125
- w_up: bfloat16 [32, 2048, 768], P('ctx'), may hold values from -0.125 to 0.125
- w_down: bfloat16 [32, 768, 2048], P('ctx'), may hold values from -0.21875 to 0.21875
Outputs:
- layer_out: bfloat16 [16384, 2048], P(('ctx', 'exp'))
Inputs may be any that keep to these rules, and one draw needn't show every extreme that they name: `expert_ids`: in each aligned block of 128 rows (the rows of one device) no expert is named by more than 40 rows, a bound that some block reaches; a row names 8 different experts.
All inputs are finite; a program needn't handle non-finite values.
Results may differ from a plain program's by a relative error of at most 0.0052.
Values may be sent and summed in bfloat16 or wider, within the bound.
A program may use at most 320 MiB of HBM per device.

v0:
```python
import jax
import jax.numpy as jnp
from jax import lax
from jax.sharding import PartitionSpec as P

D = 2048
HEADS = 32
HEAD_DIM = 64
STATE = 64
KERNEL = 4
TOPK = 8
CAP = 40


EXACT = lax.Precision.HIGHEST


def from_behind(block, axis, distance):
    devices = range(lax.axis_size(axis))
    route = [(i - distance, i) for i in devices if i - distance in devices]
    return lax.ppermute(block, axis, route)


def prefix(part, axis, combine, identity):
    place = lax.axis_index(axis)
    gathered = jax.tree.map(lambda a: lax.all_gather(a, axis), part)
    state = jax.tree.map(lambda a, e: jnp.zeros_like(a) + jnp.asarray(e, a.dtype), part, identity)

    def one(step, state):
        return combine(
            state, jax.tree.map(lambda a: lax.dynamic_index_in_dim(a, step, 0, False), gathered)
        )

    return lax.fori_loop(0, place, one, state)


def block_terms(x_block, input_map, output_map, increment_tile, decay_rate):
    count = x_block.shape[0]
    cum_log = jnp.cumsum(-increment_tile * decay_rate[:, None], axis=1)
    capacity_cells = jnp.arange(count)
    causal = capacity_cells[:, None] >= capacity_cells[None, :]
    gap_log = jnp.where(causal[None], cum_log[:, :, None] - cum_log[:, None, :], 0.0)
    inside_offset = jnp.where(causal[None], jnp.exp(gap_log), 0.0)
    cross_gram = jnp.dot(output_map, input_map.T, preferred_element_type=jnp.float32)
    mixing = inside_offset * cross_gram[None] * increment_tile[:, None, :]
    head_view = x_block.astype(jnp.float32).reshape(count, HEADS, HEAD_DIM)
    inner_y = jnp.einsum("hts,shp->thp", mixing, head_view, precision=EXACT)
    tail_w = jnp.exp(cum_log[:, -1:] - cum_log) * increment_tile
    weighted = head_view * tail_w.T[:, :, None]
    state_local = jnp.einsum(
        "shp,sn->hpn", weighted, input_map.astype(jnp.float32), precision=EXACT
    )
    return (inner_y, jnp.exp(cum_log), state_local, jnp.exp(cum_log[:, -1]), head_view)


def join_carry(earlier, later):
    return (earlier[0] * later[0], later[0][:, None, None] * earlier[1] + later[1])


def body(
    filter_entry_array,
    gate_input,
    step_unshifted,
    step_bias,
    decay_log,
    conv_weight,
    conv_bias,
    skip_gain,
    mixer_gain,
    residual,
    expert_norm,
    router_weight,
    expert_ids,
    w_gate,
    w_up,
    w_down,
):
    row_count = filter_entry_array.shape[0]
    rim_rows = from_behind(filter_entry_array[row_count - (KERNEL - 1) :], ("ctx", "exp"), 1)
    padded = jnp.concatenate([rim_rows, filter_entry_array], axis=0).astype(jnp.float32)
    summed = jnp.zeros((row_count, padded.shape[1]), jnp.float32) + conv_bias[None, :]
    for offset in range(KERNEL):
        summed = summed + conv_weight[offset][None, :] * padded[offset : offset + row_count]
    filter_result_array = jax.nn.silu(summed).astype(jnp.bfloat16)
    x_block = filter_result_array[:, :D]
    input_map = filter_result_array[:, D : D + STATE]
    output_map = filter_result_array[:, D + STATE :]
    step_size = jax.nn.softplus(step_unshifted + step_bias[:, None])
    decay_rate = jnp.exp(decay_log)
    inner_y, entry_w, state_local, through, head_view = block_terms(
        x_block, input_map, output_map, step_size, decay_rate
    )
    own_pair = (through, state_local)
    identity = (jnp.ones_like(through), jnp.zeros_like(state_local))
    before = prefix(own_pair, ("ctx", "exp"), join_carry, identity)
    carried = entry_w.T[:, :, None] * jnp.einsum(
        "tn,hpn->thp", output_map.astype(jnp.float32), before[1], precision=EXACT
    )
    direct = skip_gain[None, :, None] * head_view
    ssm_out = (inner_y + carried + direct).reshape(row_count, D)
    gated = ssm_out * jax.nn.silu(gate_input.astype(jnp.float32))
    mixer_out = (
        gated
        * lax.rsqrt(jnp.mean(gated * gated, axis=-1, keepdims=True) + 1e-05)
        * mixer_gain[None, :]
    )
    hidden_state = (residual.astype(jnp.float32) + mixer_out).astype(jnp.bfloat16)
    hidden_features = hidden_state.astype(jnp.float32)
    normed = (
        hidden_features
        * lax.rsqrt(jnp.mean(hidden_features * hidden_features, axis=-1, keepdims=True) + 1e-05)
        * expert_norm[None, :]
    ).astype(jnp.bfloat16)
    logits = jnp.dot(normed, router_weight, preferred_element_type=jnp.float32)
    score = jax.nn.sigmoid(jnp.take_along_axis(logits, expert_ids, axis=1))
    gates = score / jnp.sum(score, axis=1, keepdims=True)
    local_experts = w_gate.shape[0]
    sources = lax.axis_size("ctx")
    experts_all = local_experts * sources
    pair_count = row_count * TOPK
    flat_ids = expert_ids.reshape(pair_count)
    one_hot = (flat_ids[:, None] == jnp.arange(experts_all, dtype=jnp.int32)[None, :]).astype(
        jnp.int32
    )
    slot_of = jnp.sum((jnp.cumsum(one_hot, axis=0) - one_hot) * one_hot, axis=1)
    destination = flat_ids * CAP + slot_of
    repeated = jnp.broadcast_to(normed[:, None, :], (row_count, TOPK, D)).reshape(pair_count, D)
    outgoing = jnp.zeros((experts_all * CAP, D), jnp.bfloat16).at[destination].set(repeated)
    outgoing = outgoing.reshape(experts_all, CAP, D)
    arrived = lax.all_to_all(outgoing, "ctx", split_axis=0, concat_axis=0, tiled=True)
    slot_count = arrived.shape[1]
    grouped = arrived.reshape(sources, local_experts, slot_count, D)
    gate_val = jnp.einsum("sekd,edf->sekf", grouped, w_gate, preferred_element_type=jnp.float32)
    up_val = jnp.einsum("sekd,edf->sekf", grouped, w_up, preferred_element_type=jnp.float32)
    activated = (jax.nn.silu(gate_val) * up_val).astype(jnp.bfloat16)
    produced = jnp.einsum(
        "sekf,efd->sekd", activated, w_down, preferred_element_type=jnp.float32
    ).astype(jnp.bfloat16)
    returned = lax.all_to_all(
        produced.reshape(sources * local_experts, slot_count, D),
        "ctx",
        split_axis=0,
        concat_axis=0,
        tiled=True,
    )
    picked = (
        returned.reshape(experts_all * CAP, D)[destination]
        .astype(jnp.float32)
        .reshape(row_count, TOPK, D)
    )
    expert_sum = jnp.sum(gates[:, :, None] * picked, axis=1)
    return (hidden_features + expert_sum).astype(jnp.bfloat16)


def solution(mesh):
    return jax.shard_map(
        body,
        mesh=mesh,
        in_specs=(
            P(("ctx", "exp"), None),
            P(("ctx", "exp"), None),
            P(None, ("ctx", "exp")),
            P(),
            P(),
            P(),
            P(),
            P(),
            P(),
            P(("ctx", "exp"), None),
            P(),
            P(),
            P(("ctx", "exp"), None),
            P("ctx", None, None),
            P("ctx", None, None),
            P("ctx", None, None),
        ),
        out_specs=P(("ctx", "exp"), None),
        check_vma=False,
    )
```

profile of v0, /device:TPU:0, one launch (start us, length us, event | category | flops | bytes accessed | tf_op | source)
XLA Modules:
  0.0 864.0 jit_solution(9960007975437159111)
XLA Ops:
  6.5 0.0 copy-start
  6.5 0.0 all-gather.4.cloned.1.call-start
  6.5 0.9 slice.47
  7.5 4.0 collective-permute-start
  11.5 0.7 exp.52
  12.2 0.8 negate_multiply_fusion
  13.0 0.3 reduce_window_sum.26
  13.3 0.2 slice_reduce_fusion
  13.5 0.1 exponential_bitcast_fusion
  13.6 1.0 slice_reduce_fusion.4
  14.6 2.1 copy.48
  16.7 0.0 collective-permute-done
  16.7 1.1 copy.47
  17.7 1.7 maximum_convert_fusion
  19.4 0.0 copy-done.8
  19.4 0.0 copy-start.7
  19.4 2.8 multiply_convert_fusion
  22.3 0.0 copy-start.2
  22.3 0.7 copy-done.5
  23.0 0.2 copy-done.2
  23.2 1.7 fusion.33
  24.9 0.0 all-gather.4.cloned.1.call-update
  24.9 0.1 copy.54
  25.0 0.1 eq.29
  25.1 0.1 eq.25
  25.2 0.3 dynamic-update-slice
  25.5 67.5 %all-reduce = f32[4096]{0:T(1024)S(1)} all-reduce(f32[4096]{0:T(1024)S(1)} %dynamic-update-slice), channel_id=2, replica_groups=mesh['ctx'=32,'exp'=4] {'ctx','exp'}, use_global_device_ids=true, to_apply=%add | all-reduce | flops 4096 | bytes 32768
  93.0 0.1 reshape.203
  93.1 9.0 %reduce-window.6 = s32[32,8,128]{2,1,0:T(8,128)S(1)} reduce-window(s32[32,8,128]{2,1,0:T(8,128)S(1)} %fusion.56, s32[]{:T(128)} %constant.64.clone.1), window={size=1x1x128 pad=0_0x0_0x127_0}, to_apply=%region_6.7 | reduce-window | flops 4161536 | bytes 262148 | tf_op jit(solution)/shard_map/reduce-window
  102.1 0.1 slice.73
  102.2 0.1 copy.56
  102.3 0.1 copy.57
  102.4 0.1 copy.53
  102.5 0.1 mul.234
  102.7 0.1 broadcast_add_fusion
  102.8 0.9 fusion.60
  103.8 4.4 fusion.24
  108.2 203.0 %all-gather.4.cloned.1.call-done = f32[4096,64,64]{2,1,0:T(8,128)} async-done(((f32[32,64,64]{2,1,0:T(8,128)}), f32[4096,64,64]{2,1,0:T(8,128)}) %all-gather.4.cloned.1.call-update) | async-done | bytes 67108880 | tf_op jit(solution)/shard_map/all_gather | solution.py:26
  311.2 1.2 broadcast_in_dim.31
  312.4 0.7 copy-done.11
  313.0 3.4 fusion.28
  316.4 2.6 copy.49
  319.0 1.8 multiply_reduce_fusion
  320.8 0.0 copy-done.9
  320.8 2.1 fusion.38
  323.0 0.8 copy-done.3
  323.8 1.0 fusion.40
  324.8 10.1 %scatter_custom_fusion = bf16[1280,2048]{1,0:T(8,128)(2,1)} fusion(s32[1024]{0:T(1024)S(1)} %bitcast.123, bf16[]{:T(256)} %constant.74.clone.1, bf16[128,2048]{1,0:T(8,128)(2,1)} %fusion.40), kind=kCustom, calls=%fused_computation.7 | custom fusion | bytes 5767170 | tf_op jit(solution)/shard_map/scatter | solution.py:128
  334.8 408.7 %all_to_all.10 = bf16[32,40,2048]{2,1,0:T(8,128)(2,1)S(1)} all-to-all(bf16[32,40,2048]{2,1,0:T(8,128)(2,1)} %bitcast.115), channel_id=1, replica_groups=mesh['ctx'=32,'exp'=4] {'ctx'}, dimensions={0} | all-to-all | bytes 10485760 | tf_op jit(solution)/shard_map/all_to_all | solution.py:130
  743.5 2.3 copy-done.1
  745.8 6.4 fusion.8
  752.2 0.0 copy-done
  752.3 14.7 %convolution_convert_fusion = bf16[32,40,2048]{2,1,0:T(8,128)(2,1)} fusion(bf16[1,768,2048]{2,1,0:T(8,128)(2,1)S(1)} %copy-done, f32[32,40,768]{2,1,0:T(8,128)} %fusion.8, bf16[32,40,2048]{2,1,0:T(8,128)(2,1)} %copy-done.1, bf16[1,2048,768]{2,1,0:T(8,128)(2,1)} %param.31), kind=kOutput, calls=%fused_computation.9 | convolution fusion | flops 8061583360 | bytes 20709376 | tf_op jit(solution)/shard_map/sekf,efd->sekd/dot_general | solution.py:136
  766.9 5.3 all-to-all-start.1
  772.2 0.1 copy.50
  772.3 0.1 reshape.189
  772.4 1.3 fusion.66
  773.7 7.0 gather_fusion.1
  780.8 0.1 reshape.192
  781.0 0.1 copy.52
  781.1 56.6 %all-to-all-done.1 = bf16[32,40,2048]{2,1,0:T(8,128)(2,1)} async-done(((bf16[32,40,2048]{2,1,0:T(8,128)(2,1)}), bf16[32,40,2048]{2,1,0:T(8,128)(2,1)}, u32[]{:S(2)}, u32[]{:S(2)}) %all-to-all-start.1) | async-done | bytes 5242912 | tf_op jit(solution)/shard_map/all_to_all | solution.py:139
  837.7 12.0 %gather_fusion = bf16[1024,2048]{1,0:T(8,128)(2,1)} fusion(bf16[1280,2048]{1,0:T(8,128)(2,1)} %bitcast.32, s32[1024]{0:T(1024)S(1)} %broadcast_clamp_fusion), kind=kCustom, calls=%fused_computation | custom fusion | bytes 8392704 | tf_op jit(solution)/shard_map/gather | solution.py:147
  849.7 6.6 fusion
  856.3 0.9 fusion.41
  (32 shorter events, 0.3 us)
Async XLA Ops:
  6.5 745.7 %copy-start = (bf16[1,768,2048]{2,1,0:T(8,128)(2,1)S(1)}, bf16[1,768,2048]{2,1,0:T(8,128)(2,1)}, u32[]{:S(2)}) copy-start(bf16[1,768,2048]{2,1,0:T(8,128)(2,1)} %param.33) | copy-start | bytes 9437188
  6.5 12.9 %copy-start.8 = (f32[2176]{0:T(1024)S(1)}, f32[2176]{0:T(1024)}, u32[]{:S(2)}) copy-start(f32[2176]{0:T(1024)} %param.24) | copy-start | bytes 26116
  6.5 304.7 %all-gather.4.cloned.1.call-start = ((), (), s32[]{:S(2)}) async-start(), calls=%async_computation.2 | async-start | bytes 135266304 | tf_op jit(solution)/shard_map/all_gather | solution.py:26
  7.5 9.2 %collective-permute-start = (bf16[3,2176]{1,0:T(4,128)(2,1)S(1)}, bf16[3,2176]{1,0:T(4,128)(2,1)S(1)}, u32[]{:S(2)}, u32[]{:S(2)}) collective-permute-start(bf16[3,2176]{1,0:T(4,128)(2,1)S(1)} %slice.47), channel_id=1, source_target_pairs={{0,1},{1,2},{2,3},{3,4},{4,5},{5,6},{6,7},{7,8},{8,9},{9,10},{10,1... | collective-permute-start | bytes 39176 | tf_op jit(solution)/shard_map/ppermute | solution.py:21
  19.4 5.5 copy-start.7
  22.2 0.8 copy-start.5
  22.3 0.9 copy-start.2
  312.4 0.7 copy-start.11
  313.0 7.8 copy-start.9
  316.4 7.4 copy-start.10
  323.0 0.8 copy-start.3
  334.8 411.0 %copy-start.12 = (bf16[1,2048,768]{2,1,0:T(8,128)(2,1)S(1)}, bf16[1,2048,768]{2,1,0:T(8,128)(2,1)}, u32[]{:S(2)}) copy-start(bf16[1,2048,768]{2,1,0:T(8,128)(2,1)} %param.32) | copy-start | bytes 9437188
  743.5 2.3 copy-start.1
  766.9 5.5 copy-start.6
  766.9 70.8 %all-to-all-start.1 = ((bf16[32,40,2048]{2,1,0:T(8,128)(2,1)}), bf16[32,40,2048]{2,1,0:T(8,128)(2,1)}, u32[]{:S(2)}, u32[]{:S(2)}) async-start(bf16[32,40,2048]{2,1,0:T(8,128)(2,1)} %convolution_convert_fusion), calls=%async_computation.1 | async-start | bytes 10485760 | tf_op jit(solution)/shard_map/all_to_all | solution.py:139
  849.7 6.6 copy-start.4
Sparse Core Ops, SparseCore 0:
  25.0 286.1 all-gather.3
where the time goes:
time: 874 us; the launch traced here: 864 us
  blocking collectives  476 us (54%)
  waiting for transfers between devices  260 us (30%)
  local copies, waits for them, and re-layouts  45.1 us (5%)
  matrix products  32.8 us (4%)
  other arithmetic  27.3 us (3%)
  between operations  13.7 us (2%)
  starting transfers between devices  9.3 us (1%)
    all_to_all x1, blocking collectives, body(): lax.all_to_all(outgoing, 'ctx', split_axis=0, concat_axis=0, tiled=True)  409 us
    all_gather x1, waiting for transfers between devices, prefix(): gathered = jax.tree.map(lambda a: lax.all_gather(a, axis), part)  203 us
    unnamed x1, blocking collectives  67.5 us
    all_to_all x1, waiting for transfers between devices, body(): lax.all_to_all(produced.reshape(sources * local_experts, slot_count, D),...  56.6 us
  transfers between devices with their start and end apart: 3, of which 2 were waited for; matrix products, arithmetic and copies ran while one was open for 3% of the time, Pallas kernels for 0%

commit v1 on v0

--- a/solution.py
+++ b/solution.py
@@ -21,17 +21,25 @@
     return lax.ppermute(block, axis, route)
 
 
-def prefix(part, axis, combine, identity):
-    place = lax.axis_index(axis)
-    gathered = jax.tree.map(lambda a: lax.all_gather(a, axis), part)
-    state = jax.tree.map(lambda a, e: jnp.zeros_like(a) + jnp.asarray(e, a.dtype), part, identity)
-
-    def one(step, state):
-        return combine(
-            state, jax.tree.map(lambda a: lax.dynamic_index_in_dim(a, step, 0, False), gathered)
-        )
-
-    return lax.fori_loop(0, place, one, state)
+def prefix(state_local, log_through):
+    axes = ("ctx", "exp")
+    devices = lax.axis_size(axes)
+    share = HEADS * HEAD_DIM * STATE // devices
+    per_head = devices // HEADS
+    pieces = state_local.reshape(devices, share)
+    logs = jnp.repeat(log_through, per_head)[:, None]
+    packed = jnp.concatenate([pieces, jnp.broadcast_to(logs, (devices, 128))], axis=1)
+    arrived = lax.all_to_all(packed, axes, split_axis=0, concat_axis=0, tiled=True)
+    states, log = arrived[:, :share], arrived[:, share]
+    place = jnp.arange(devices)
+    lower = place[:, None] > place[None, :]
+    gap = jnp.dot(
+        jnp.where(lower, log[None, :], 0.0), lower.astype(jnp.float32), precision=EXACT
+    )
+    weight = jnp.where(lower, jnp.exp(jnp.minimum(gap, 0.0)), 0.0)
+    before = jnp.dot(weight, states, precision=EXACT)
+    back = lax.all_to_all(before, axes, split_axis=0, concat_axis=0, tiled=True)
+    return back.reshape(HEADS, HEAD_DIM, STATE)
 
 
 def block_terms(x_block, input_map, output_map, increment_tile, decay_rate):
@@ -50,11 +58,7 @@
     state_local = jnp.einsum(
         "shp,sn->hpn", weighted, input_map.astype(jnp.float32), precision=EXACT
     )
-    return (inner_y, jnp.exp(cum_log), state_local, jnp.exp(cum_log[:, -1]), head_view)
-
-
-def join_carry(earlier, later):
-    return (earlier[0] * later[0], later[0][:, None, None] * earlier[1] + later[1])
+    return (inner_y, jnp.exp(cum_log), state_local, cum_log[:, -1], head_view)
 
 
 def body(
@@ -90,11 +94,9 @@
     inner_y, entry_w, state_local, through, head_view = block_terms(
         x_block, input_map, output_map, step_size, decay_rate
     )
-    own_pair = (through, state_local)
-    identity = (jnp.ones_like(through), jnp.zeros_like(state_local))
-    before = prefix(own_pair, ("ctx", "exp"), join_carry, identity)
+    before = prefix(state_local, through)
     carried = entry_w.T[:, :, None] * jnp.einsum(
-        "tn,hpn->thp", output_map.astype(jnp.float32), before[1], precision=EXACT
+        "tn,hpn->thp", output_map.astype(jnp.float32), before, precision=EXACT
     )
     direct = skip_gain[None, :, None] * head_view
     ssm_out = (inner_y + carried + direct).reshape(row_count, D)

time: 874 us -> 280 us (0.32); the launches traced: 864 us -> 279 us
  blocking collectives: 476 us -> 66.6 us
  waiting for transfers between devices: 260 us -> 67.5 us
  starting transfers between devices: 9.3 us -> 27.1 us
  between operations: 13.7 us -> 0.34 us
    all_to_all x1, blocking collectives: 409 us -> 66.6 us  [body(): lax.all_to_all(outgoing, 'ctx', split_axis=0, concat_axis=0, tiled=True)]
    all_gather x1 -> x0, waiting for transfers between devices: 203 us -> none  [prefix(): gathered = jax.tree.map(lambda a: lax.all_gather(a, axis), part)]
    unnamed x1 -> x0, blocking collectives: 67.5 us -> none
    all_to_all x0 -> x2, starting transfers between devices: none -> 17.8 us  [the longest x1 11.1 us: prefix(): lax.all_to_all(packed, axes, split_axis=0, concat_axis=0, tiled=True)]
    all_to_all x0 -> x2, waiting for transfers between devices: none -> 10.9 us  [the longest x1 7.23 us: prefix(): back = lax.all_to_all(before, axes, split_axis=0, concat_axis=0, tiled=True)]
  transfers between devices with their start and end apart: 3 -> 4, of which waited for: 2 -> 3; matrix products, arithmetic and copies ran while one was open for 3% -> 11% of each run, Pallas kernels for 0% -> 0%
where the time goes in v1:
time: 280 us; the launch traced here: 279 us
  waiting for transfers between devices  67.5 us (24%)
  blocking collectives  66.6 us (24%)
  local copies, waits for them, and re-layouts  52.4 us (19%)
  matrix products  33.6 us (12%)
  other arithmetic  31.5 us (11%)
  starting transfers between devices  27.1 us (10%)
    all_to_all x1, blocking collectives, body(): lax.all_to_all(outgoing, 'ctx', split_axis=0, concat_axis=0, tiled=True)  66.6 us
    all_to_all x1, waiting for transfers between devices, body(): lax.all_to_all(produced.reshape(sources * local_experts, slot_count, D),...  56.6 us
    dot_general x1, matrix products, body(): jnp.einsum('sekf,efd->sekd', activated, w_down, preferred_element_type=jn...  14.7 us
    gather x1, local copies, waits for them, and re-layouts, body(): returned.reshape(experts_all * CAP, D)[destination].astype(jnp.float32)  12 us
    all_to_all x1, starting transfers between devices, prefix(): lax.all_to_all(packed, axes, split_axis=0, concat_axis=0, tiled=True)  11.1 us
    scatter x1, local copies, waits for them, and re-layouts, body(): jnp.zeros((experts_all * CAP, D), jnp.bfloat16).at[destination]  10.1 us
    another operation x3, other arithmetic  9.14 us
    unnamed x29, local copies, waits for them, and re-layouts  8.06 us
  transfers between devices with their start and end apart: 4, of which 3 were waited for; matrix products, arithmetic and copies ran while one was open for 11% of the time, Pallas kernels for 0%

profile of v1, /device:TPU:0, one launch (start us, length us, event | category | flops | bytes accessed | tf_op | source)
XLA Modules:
  0.0 279.0 jit_solution(7917547051941733708)
XLA Ops:
  0.0 0.9 slice.53
  0.9 4.0 %collective-permute-start = (bf16[3,2176]{1,0:T(4,128)(2,1)S(1)}, bf16[3,2176]{1,0:T(4,128)(2,1)S(1)}, u32[]{:S(2)}, u32[]{:S(2)}) collective-permute-start(bf16[3,2176]{1,0:T(4,128)(2,1)S(1)} %slice.53), channel_id=1, source_target_pairs={{0,1},{1,2},{2,3},{3,4},{4,5},{5,6},{6,7},{7,8},{8,9},{9,10},{10,1... | collective-permute-start | bytes 39176 | tf_op jit(solution)/shard_map/ppermute | solution.py:21
  5.0 0.7 exp.42
  5.7 0.8 negate_multiply_fusion
  6.5 0.3 reduce_window_sum.26
  6.8 0.2 slice_reduce_fusion.1
  6.9 0.8 copy.72
  7.7 0.1 eq.29
  7.8 0.1 exponential_bitcast_fusion
  7.9 1.0 slice_reduce_fusion.5
  9.0 2.1 copy.65
  11.1 0.1 broadcast_in_dim.51
  11.2 1.1 copy.64
  12.3 1.7 maximum_convert_fusion
  14.0 2.8 multiply_convert_fusion
  16.8 0.7 copy-done.5
  17.6 0.2 copy-done.2
  17.7 1.6 fusion.35
  19.4 2.3 reshape.170
  21.8 1.1 pad_maximum_fusion
  22.9 1.2 all_to_all.20
  24.1 11.1 %all-to-all-start = ((f32[128,1,1152]{2,1,0:T(1,128)}), f32[128,1,1152]{2,1,0:T(1,128)}, u32[]{:S(2)}, u32[]{:S(2)}) async-start(f32[128,1,1152]{2,1,0:T(1,128)} %all_to_all.20), calls=%async_computation | async-start | bytes 1179648 | tf_op jit(solution)/shard_map/all_to_all | solution.py:32
  35.2 0.1 eq.25
  35.3 0.1 copy.71
  35.4 0.1 mul.215
  35.5 9.0 %reduce-window.6 = s32[32,8,128]{2,1,0:T(8,128)S(1)} reduce-window(s32[32,8,128]{2,1,0:T(8,128)S(1)} %fusion.59, s32[]{:T(128)} %constant.32.clone.1), window={size=1x1x128 pad=0_0x0_0x127_0}, to_apply=%region_4.5 | reduce-window | flops 4161536 | bytes 262148 | tf_op jit(solution)/shard_map/reduce-window
  44.5 0.1 slice.83
  44.6 0.1 copy.74
  44.8 0.1 copy.75
  44.9 0.1 broadcast_add_fusion
  45.0 3.7 %all-to-all-done = f32[128,1,1152]{2,1,0:T(1,128)} async-done(((f32[128,1,1152]{2,1,0:T(1,128)}), f32[128,1,1152]{2,1,0:T(1,128)}, u32[]{:S(2)}, u32[]{:S(2)}) %all-to-all-start) | async-done | bytes 589856 | tf_op jit(solution)/shard_map/all_to_all | solution.py:32
  48.8 1.1 copy.80
  49.9 0.1 slice_reduce_fusion
  50.0 0.2 fusion.30
  50.2 0.6 convolution_bitcast_fusion
  50.8 1.4 copy.66
  52.1 6.7 %all-to-all-start.1 = ((f32[128,1,1024]{2,1,0:T(1,128)}), f32[128,1,1024]{2,1,0:T(1,128)}, u32[]{:S(2)}, u32[]{:S(2)}) async-start(f32[128,1,1024]{2,1,0:T(1,128)} %copy.66), calls=%async_computation.1 | async-start | bytes 1048576 | tf_op jit(solution)/shard_map/all_to_all | solution.py:41
  58.8 0.9 fusion.66
  59.8 4.4 %fusion.24 = f32[128,32,64]{0,2,1:T(8,128)} fusion(bf16[128,32,64]{0,2,1:T(8,128)(2,1)} %bitcast.115, f32[32,128]{1,0:T(8,128)S(1)} %get-tuple-element.12, f32[128,128]{1,0:T(8,128)S(1)} %fusion.66, f32[32,128]{1,0:T(8,128)S(1)} %reduce_window_sum.26, pred[128,128]{1,0:T(8,128)(4,1)S(1)} %iota_compare_fusion.3), kind=kOutput, calls=%fused_computation.33 | convolution fusion | flops 405274624 | bytes 1687552 | tf_op jit(solution)/shard_map/hts,shp->thp/dot_general | solution.py:55
  64.2 7.2 %all-to-all-done.1 = f32[128,1,1024]{2,1,0:T(1,128)} async-done(((f32[128,1,1024]{2,1,0:T(1,128)}), f32[128,1,1024]{2,1,0:T(1,128)}, u32[]{:S(2)}, u32[]{:S(2)}) %all-to-all-start.1) | async-done | bytes 524320 | tf_op jit(solution)/shard_map/all_to_all | solution.py:41
  71.4 3.1 %reduce.6 = f32[128,1024]{1,0:T(8,128)} reduce(f32[128,1,1024]{2,1,0:T(1,128)} %all-to-all-done.1, f32[]{:T(128)} %constant.66), dimensions={1}, to_apply=%all_to_all.24.reduce_sub_computation | reduce | bytes 1048580 | tf_op jit(solution)/shard_map/all_to_all | solution.py:41
  74.5 2.4 reshape.171
  76.9 3.4 %fusion.28 = f32[128,32,64]{0,2,1:T(8,128)} fusion(f32[128,32,64]{0,2,1:T(8,128)} %fusion.24, f32[32,64,64]{2,1,0:T(8,128)} %reshape.171, bf16[128,32,64]{0,2,1:T(8,128)(2,1)} %bitcast.116, f32[32]{0:T(128)S(1)} %copy-done.11, f32[128,32]{0,1:T(8,128)S(1)} %get-tuple-element.13, bf16[128,2176]{0,1:T(8,128)(2,1)} %copy-done.5), kind=kOutput, calls=%fused_computation.36 | convolution fusion | flops 202637312 | bytes 3702912 | tf_op jit(solution)/shard_map/tn,hpn->thp/dot_general | solution.py:98
  80.3 2.6 copy.67
  82.9 1.8 multiply_reduce_fusion
  84.7 2.1 fusion.40
  86.9 0.8 copy-done.3
  87.7 1.0 fusion.42
  88.6 10.1 %scatter_custom_fusion = bf16[1280,2048]{1,0:T(8,128)(2,1)} fusion(s32[1024]{0:T(1024)S(1)} %bitcast.123, bf16[]{:T(256)} %constant.47.clone.1, bf16[128,2048]{1,0:T(8,128)(2,1)} %fusion.42), kind=kCustom, calls=%fused_computation.5 | custom fusion | bytes 5767170 | tf_op jit(solution)/shard_map/scatter | solution.py:130
  98.7 66.6 %all_to_all.31 = bf16[32,40,2048]{2,1,0:T(8,128)(2,1)S(1)} all-to-all(bf16[32,40,2048]{2,1,0:T(8,128)(2,1)} %bitcast.113), channel_id=1, replica_groups=mesh['ctx'=32,'exp'=4] {'ctx'}, dimensions={0} | all-to-all | bytes 10485760 | tf_op jit(solution)/shard_map/all_to_all | solution.py:132
  165.3 2.3 copy-done.1
  167.7 6.4 %fusion.8 = f32[32,40,768]{2,1,0:T(8,128)} fusion(bf16[32,40,2048]{2,1,0:T(8,128)(2,1)S(1)} %all_to_all.31, bf16[1,2048,768]{2,1,0:T(8,128)(2,1)S(1)} %copy-done.12), kind=kOutput, calls=%fused_computation.16 | convolution fusion | flops 4026531840 | bytes 12320768 | tf_op jit(solution)/shard_map/sekd,edf->sekf/dot_general | solution.py:136
  174.1 14.7 %convolution_convert_fusion = bf16[32,40,2048]{2,1,0:T(8,128)(2,1)} fusion(bf16[1,768,2048]{2,1,0:T(8,128)(2,1)S(1)} %copy-done, f32[32,40,768]{2,1,0:T(8,128)} %fusion.8, bf16[32,40,2048]{2,1,0:T(8,128)(2,1)} %copy-done.1, bf16[1,2048,768]{2,1,0:T(8,128)(2,1)} %param.29), kind=kOutput, calls=%fused_computation.7 | convolution fusion | flops 8061583360 | bytes 20709376 | tf_op jit(solution)/shard_map/sekf,efd->sekd/dot_general | solution.py:138
  188.8 5.3 %all-to-all-start.3 = ((bf16[32,40,2048]{2,1,0:T(8,128)(2,1)}), bf16[32,40,2048]{2,1,0:T(8,128)(2,1)}, u32[]{:S(2)}, u32[]{:S(2)}) async-start(bf16[32,40,2048]{2,1,0:T(8,128)(2,1)} %convolution_convert_fusion), calls=%async_computation.3 | async-start | bytes 10485760 | tf_op jit(solution)/shard_map/all_to_all | solution.py:141
  194.1 0.1 copy.68
  194.2 0.1 reshape.191
  194.3 1.3 fusion.73
  195.6 7.0 %gather_fusion.1 = f32[1024]{0:T(1024)S(1)} fusion(f32[128,32]{0,1:T(8,128)S(1)} %fusion.73, s32[1024]{0:T(1024)S(1)} %reshape.191), kind=kCustom, calls=%fused_computation.1 | custom fusion | bytes 16384 | tf_op jit(solution)/shard_map/jit(take_along_axis)/gather | solution.py:117
  202.6 0.1 reshape.194
  202.9 0.1 copy.70
  203.0 56.6 %all-to-all-done.3 = bf16[32,40,2048]{2,1,0:T(8,128)(2,1)} async-done(((bf16[32,40,2048]{2,1,0:T(8,128)(2,1)}), bf16[32,40,2048]{2,1,0:T(8,128)(2,1)}, u32[]{:S(2)}, u32[]{:S(2)}) %all-to-all-start.3) | async-done | bytes 5242912 | tf_op jit(solution)/shard_map/all_to_all | solution.py:141
  259.5 12.0 %gather_fusion = bf16[1024,2048]{1,0:T(8,128)(2,1)} fusion(bf16[1280,2048]{1,0:T(8,128)(2,1)} %bitcast.30, s32[1024]{0:T(1024)S(1)} %broadcast_clamp_fusion), kind=kCustom, calls=%fused_computation | custom fusion | bytes 8392704 | tf_op jit(solution)/shard_map/gather | solution.py:149
  271.5 6.6 %fusion = f32[128,2048]{1,0:T(8,128)S(1)} fusion(bf16[1024,2048]{1,0:T(8,128)(2,1)} %gather_fusion, f32[128,8]{1,0:T(8,128)S(1)} %copy.70), kind=kLoop, calls=%fused_computation.4 | loop fusion | flops 6029312 | bytes 5246976 | tf_op jit(solution)/shard_map/reduce_sum | solution.py:153
  278.1 0.9 fusion.43
  (40 shorter events, 0.5 us)
Async XLA Ops:
  0.0 174.1 %copy-start = (bf16[1,768,2048]{2,1,0:T(8,128)(2,1)S(1)}, bf16[1,768,2048]{2,1,0:T(8,128)(2,1)}, u32[]{:S(2)}) copy-start(bf16[1,768,2048]{2,1,0:T(8,128)(2,1)} %param.31) | copy-start | bytes 9437188
  0.0 14.0 %copy-start.8 = (f32[2176]{0:T(1024)S(1)}, f32[2176]{0:T(1024)}, u32[]{:S(2)}) copy-start(f32[2176]{0:T(1024)} %param.22) | copy-start | bytes 26116
  0.9 10.3 %collective-permute-start = (bf16[3,2176]{1,0:T(4,128)(2,1)S(1)}, bf16[3,2176]{1,0:T(4,128)(2,1)S(1)}, u32[]{:S(2)}, u32[]{:S(2)}) collective-permute-start(bf16[3,2176]{1,0:T(4,128)(2,1)S(1)} %slice.53), channel_id=1, source_target_pairs={{0,1},{1,2},{2,3},{3,4},{4,5},{5,6},{6,7},{7,8},{8,9},{9,10},{10,1... | collective-permute-start | bytes 39176 | tf_op jit(solution)/shard_map/ppermute | solution.py:21
  16.8 0.8 copy-start.5
  16.8 0.9 copy-start.2
  17.7 17.5 %copy-start.7 = (s32[128,8]{0,1:T(8,128)S(1)}, s32[128,8]{0,1:T(8,128)}, u32[]{:S(2)}) copy-start(s32[128,8]{0,1:T(8,128)} %param.28) | copy-start | bytes 12292
  24.1 24.6 %all-to-all-start = ((f32[128,1,1152]{2,1,0:T(1,128)}), f32[128,1,1152]{2,1,0:T(1,128)}, u32[]{:S(2)}, u32[]{:S(2)}) async-start(f32[128,1,1152]{2,1,0:T(1,128)} %all_to_all.20), calls=%async_computation | async-start | bytes 1179648 | tf_op jit(solution)/shard_map/all_to_all | solution.py:32
  52.1 19.3 %all-to-all-start.1 = ((f32[128,1,1024]{2,1,0:T(1,128)}), f32[128,1,1024]{2,1,0:T(1,128)}, u32[]{:S(2)}, u32[]{:S(2)}) async-start(f32[128,1,1024]{2,1,0:T(1,128)} %copy.66), calls=%async_computation.1 | async-start | bytes 1048576 | tf_op jit(solution)/shard_map/all_to_all | solution.py:41
  59.8 17.1 %copy-start.11 = (f32[32]{0:T(128)S(1)}, f32[32]{0:T(128)}, u32[]{:S(2)}) copy-start(f32[32]{0:T(128)} %param.23) | copy-start | bytes 388
  76.9 7.8 %copy-start.9 = (f32[2048]{0:T(1024)S(1)}, f32[2048]{0:T(1024)}, u32[]{:S(2)}) copy-start(f32[2048]{0:T(1024)} %param.24) | copy-start | bytes 24580
  80.2 7.4 %copy-start.10 = (f32[2048]{0:T(1024)S(1)}, f32[2048]{0:T(1024)}, u32[]{:S(2)}) copy-start(f32[2048]{0:T(1024)} %param.26) | copy-start | bytes 24580
  86.9 0.8 copy-start.3
  98.7 69.0 %copy-start.12 = (bf16[1,2048,768]{2,1,0:T(8,128)(2,1)S(1)}, bf16[1,2048,768]{2,1,0:T(8,128)(2,1)}, u32[]{:S(2)}) copy-start(bf16[1,2048,768]{2,1,0:T(8,128)(2,1)} %param.30) | copy-start | bytes 9437188
  165.3 2.3 copy-start.1
  188.8 5.5 %copy-start.6 = (bf16[2048,32]{0,1:T(8,128)(2,1)S(1)}, bf16[2048,32]{0,1:T(8,128)(2,1)}, u32[]{:S(2)}) copy-start(bf16[2048,32]{0,1:T(8,128)(2,1)} %param.27) | copy-start | bytes 393220
  188.8 70.8 %all-to-all-start.3 = ((bf16[32,40,2048]{2,1,0:T(8,128)(2,1)}), bf16[32,40,2048]{2,1,0:T(8,128)(2,1)}, u32[]{:S(2)}, u32[]{:S(2)}) async-start(bf16[32,40,2048]{2,1,0:T(8,128)(2,1)} %convolution_convert_fusion), calls=%async_computation.3 | async-start | bytes 10485760 | tf_op jit(solution)/shard_map/all_to_all | solution.py:141
  271.5 6.6 %copy-start.4 = (bf16[128,2048]{1,0:T(8,128)(2,1)S(1)}, bf16[128,2048]{1,0:T(8,128)(2,1)}, u32[]{:S(2)}) copy-start(bf16[128,2048]{1,0:T(8,128)(2,1)} %copy-done.3) | copy-start | bytes 1572868

commit v2 on v1

--- a/solution.py
+++ b/solution.py
@@ -1,6 +1,8 @@
 import jax
 import jax.numpy as jnp
 from jax import lax
+from jax.experimental import pallas as pl
+from jax.experimental.pallas import tpu as pltpu
 from jax.sharding import PartitionSpec as P
 
 D = 2048
@@ -59,6 +61,386 @@
         "shp,sn->hpn", weighted, input_map.astype(jnp.float32), precision=EXACT
     )
     return (inner_y, jnp.exp(cum_log), state_local, cum_log[:, -1], head_view)
+
+
+MESH = pl.DeviceIdType.MESH
+BLOCK = 128
+PICK = 4 * CAP
+WIDE = 4 * BLOCK
+
+
+def moe_kernel(
+    normed,
+    gates,
+    hidden,
+    w_gate,
+    w_up,
+    w_down,
+    out,
+    rows,
+    meta,
+    wg,
+    wu,
+    wd,
+    picked,
+    lent,
+    activated,
+    own_y,
+    lent_y,
+    back_y,
+    select,
+    gate_col,
+    part,
+    land,
+    w_sem,
+    row_send,
+    row_recv,
+    meta_send,
+    meta_recv,
+    lent_send,
+    lent_recv,
+    back_send,
+    back_recv,
+    sum_send,
+    sum_recv,
+):
+    ctx = lax.axis_index("ctx")
+    depth = lax.axis_index("exp")
+    core = ctx % 2
+    x = (ctx // 2) % 4
+    y = ctx // 8
+    sibling = ctx + 1 - 2 * core
+
+    def device(first, second):
+        to_y = (y + core * first + (1 - core) * second + 4) % 4
+        to_x = (x + core * second + (1 - core) * first + 4) % 4
+        return ((to_y * 4 + to_x) * 2 + core, depth)
+
+    forth = (device(1, 0), device(0, 1))
+    back = (device(-1, 0), device(0, -1))
+    across = (sibling, depth)
+
+    fetch = [
+        pltpu.make_async_copy(src.at[0], dst, w_sem.at[i])
+        for i, (src, dst) in enumerate(((w_gate, wg), (w_up, wu), (w_down, wd)))
+    ]
+    for copy in fetch:
+        copy.start()
+
+    barrier = pltpu.get_barrier_semaphore()
+    partners = (*forth, *back, across)
+    for partner in partners:
+        pl.semaphore_signal(barrier, inc=1, device_id=partner, device_id_type=MESH)
+
+    rows[0:BLOCK] = normed[...]
+    meta[0] = gates[...]
+    pl.semaphore_wait(barrier, len(partners))
+
+    def remote(src, dst, send, recv, to):
+        return pltpu.make_async_remote_copy(
+            src_ref=src, dst_ref=dst, send_sem=send, recv_sem=recv, device_id=to, device_id_type=MESH
+        )
+
+    def ring(stage):
+        return (0, 4, 0) if stage == 0 else (4 * (stage - 1), 1, 1)
+
+    def row_copy(stage, kind):
+        base, stride, axis = ring(stage)
+        sem = 4 * stage + kind
+        to = (forth, back)[kind % 2][axis]
+        source, target, low, count = (
+            (0, 1, 0, BLOCK),
+            (0, 3, 0, BLOCK),
+            (1, 2, 0, BLOCK // 2),
+            (3, 2, BLOCK // 2, BLOCK // 2),
+        )[kind]
+        return remote(
+            rows.at[pl.ds((base + stride * source) * BLOCK + low, count)],
+            rows.at[pl.ds((base + stride * target) * BLOCK + low, count)],
+            row_send.at[sem],
+            row_recv.at[sem],
+            to,
+        )
+
+    def meta_copy(stage, kind):
+        base, stride, axis = ring(stage)
+        sem = 3 * stage + kind
+        source, target, to = ((0, 1, forth), (0, 3, back), (1, 2, forth))[kind]
+        return remote(
+            meta.at[base + stride * source],
+            meta.at[base + stride * target],
+            meta_send.at[sem],
+            meta_recv.at[sem],
+            to[axis],
+        )
+
+    def sum_copy(stage, kind):
+        base, stride, axis = ring(stage)
+        sem = 4 * stage + kind
+        to = (back, forth)[kind % 2][axis]
+        source, low, count, place = (
+            (2, 0, BLOCK // 2, 0),
+            (2, BLOCK // 2, BLOCK // 2, BLOCK // 2),
+            (1, 0, BLOCK, BLOCK),
+            (3, 0, BLOCK, 2 * BLOCK),
+        )[kind]
+        return remote(
+            part.at[pl.ds((base + stride * source) * BLOCK + low, count)],
+            land.at[pl.ds(stage * 3 * BLOCK + place, count)],
+            sum_send.at[sem],
+            sum_recv.at[sem],
+            to,
+        )
+
+    def lent_copy(k):
+        return remote(
+            lent.at[k], picked.at[k, pl.ds(PICK, PICK)], lent_send.at[k], lent_recv.at[k], across
+        )
+
+    def back_copy(k):
+        return remote(lent_y.at[k], back_y.at[k], back_send.at[k], back_recv.at[k], across)
+
+    def spread(stage):
+        for kind in (0, 1):
+            meta_copy(stage, kind).start()
+            row_copy(stage, kind).start()
+
+    def pass_on(stage, kind):
+        row_copy(stage, kind).wait_recv()
+        meta_copy(stage, kind).wait_recv()
+        if kind == 0:
+            meta_copy(stage, 2).start()
+        row_copy(stage, kind + 2).start()
+
+    def arrive_last(stage):
+        meta_copy(stage, 2).wait_recv()
+        row_copy(stage, 2).wait_recv()
+        row_copy(stage, 3).wait_recv()
+
+    before = (
+        lax.broadcasted_iota(jnp.int32, (BLOCK, BLOCK), 0)
+        < lax.broadcasted_iota(jnp.int32, (BLOCK, BLOCK), 1)
+    ).astype(jnp.bfloat16)
+    slot_row = lax.broadcasted_iota(jnp.int32, (PICK, WIDE), 0).astype(jnp.float32)
+
+    def choose(k):
+        gate = jnp.concatenate(
+            [
+                meta[4 * k + j, pl.ds(expert, 1), :]
+                for expert in (ctx, sibling)
+                for j in range(4)
+            ],
+            axis=0,
+        )
+        live = gate > 0.0
+        rank = jnp.dot(
+            live.astype(jnp.bfloat16), before, preferred_element_type=jnp.float32
+        )
+        shift = (lax.broadcasted_iota(jnp.int32, (8, BLOCK), 0) % 4).astype(jnp.float32) * CAP
+        slot = jnp.where(live, rank + shift, -1.0)
+        for half in range(2):
+            lanes = jnp.concatenate([slot[4 * half + j : 4 * half + j + 1] for j in range(4)], axis=1)
+            value = jnp.concatenate([gate[4 * half + j : 4 * half + j + 1] for j in range(4)], axis=1)
+            hit = slot_row == lanes
+            span = pl.ds(half * PICK, PICK)
+            select[k, span, :] = jnp.where(hit, 1.0, 0.0).astype(jnp.bfloat16)
+            total = jnp.sum(jnp.where(hit, value, 0.0), axis=1, keepdims=True)
+            gate_col[k, span, :] = jnp.broadcast_to(total, (PICK, BLOCK))
+
+        @pl.loop(0, 8)
+        def _(n):
+            cols = pl.ds(pl.multiple_of(n * 256, 256), 256)
+            got = jnp.dot(
+                select[k], rows[pl.ds(k * WIDE, WIDE), cols], preferred_element_type=jnp.float32
+            ).astype(jnp.bfloat16)
+            picked[k, pl.ds(0, PICK), cols] = got[:PICK]
+            lent[k, :, cols] = got[PICK:]
+
+        lent_copy(k).start()
+
+    def feed(k):
+        lent_copy(k).wait_recv()
+
+        @pl.loop(0, 3)
+        def _(f):
+            cols = pl.ds(pl.multiple_of(f * 256, 256), 256)
+            gate = jnp.dot(picked[k], wg[:, cols], preferred_element_type=jnp.float32)
+            up = jnp.dot(picked[k], wu[:, cols], preferred_element_type=jnp.float32)
+            activated[:, cols] = (gate * jax.nn.sigmoid(gate) * up).astype(jnp.bfloat16)
+
+        @pl.loop(0, 8)
+        def _(n):
+            cols = pl.ds(pl.multiple_of(n * 256, 256), 256)
+            made = jnp.dot(activated[...], wd[:, cols], preferred_element_type=jnp.float32)
+            scale = gate_col[k, pl.ds(0, PICK), :]
+            own_y[:, cols] = (
+                made[:PICK] * jnp.concatenate([scale, scale], axis=1)
+            ).astype(jnp.bfloat16)
+            lent_y[k, :, cols] = made[PICK:].astype(jnp.bfloat16)
+
+        back_copy(k).start()
+
+    def combine(k):
+        back_copy(k).wait_recv()
+
+        @pl.loop(0, 8)
+        def _(n):
+            cols = pl.ds(pl.multiple_of(n * 256, 256), 256)
+            scale = gate_col[k, pl.ds(PICK, PICK), :]
+            other = (
+                back_y[k, :, cols].astype(jnp.float32) * jnp.concatenate([scale, scale], axis=1)
+            ).astype(jnp.bfloat16)
+            both = jnp.concatenate([own_y[:, cols], other], axis=0)
+            part[pl.ds(k * WIDE, WIDE), cols] = lax.dot_general(
+                select[k], both, (((0,), (0,)), ((), ())), preferred_element_type=jnp.float32
+            ).astype(jnp.bfloat16)
+
+    def add_into(block, low, count, places):
+        @pl.loop(0, count // 16)
+        def _(i):
+            span = pl.ds(pl.multiple_of(block * BLOCK + low + i * 16, 16), 16)
+            total = part[span, :].astype(jnp.float32)
+            for place in places:
+                total += land[pl.ds(pl.multiple_of(place + i * 16, 16), 16), :].astype(jnp.float32)
+            part[span, :] = total.astype(jnp.bfloat16)
+
+    def sum_first(stage):
+        sum_copy(stage, 0).start()
+        sum_copy(stage, 1).start()
+
+    def sum_second(stage):
+        base, stride, _ = ring(stage)
+        place = stage * 3 * BLOCK
+        sum_copy(stage, 0).wait_recv()
+        add_into(base + stride, 0, BLOCK // 2, (place,))
+        sum_copy(stage, 2).start()
+        sum_copy(stage, 1).wait_recv()
+        add_into(base + 3 * stride, BLOCK // 2, BLOCK // 2, (place + BLOCK // 2,))
+        sum_copy(stage, 3).start()
+
+    def sum_last(stage):
+        base, _, _ = ring(stage)
+        place = stage * 3 * BLOCK
+        sum_copy(stage, 2).wait_recv()
+        sum_copy(stage, 3).wait_recv()
+        if stage > 0:
+            add_into(base, 0, BLOCK, (place + BLOCK, place + 2 * BLOCK))
+
+    spread(0)
+    spread(1)
+    pass_on(0, 0)
+    spread(2)
+    pass_on(0, 1)
+    spread(4)
+    pass_on(1, 0)
+    pass_on(1, 1)
+    arrive_last(0)
+    spread(3)
+    arrive_last(1)
+    choose(0)
+    pass_on(2, 0)
+    pass_on(2, 1)
+    for copy in fetch:
+        copy.wait()
+    feed(0)
+    pass_on(4, 0)
+    pass_on(4, 1)
+    arrive_last(2)
+    choose(1)
+    combine(0)
+    sum_first(1)
+    feed(1)
+    pass_on(3, 0)
+    pass_on(3, 1)
+    arrive_last(4)
+    choose(3)
+    combine(1)
+    sum_first(2)
+    sum_second(1)
+    feed(3)
+    sum_last(1)
+    sum_second(2)
+    arrive_last(3)
+    choose(2)
+    combine(3)
+    sum_first(4)
+    feed(2)
+    sum_last(2)
+    sum_second(4)
+    combine(2)
+    sum_first(3)
+    sum_last(4)
+    sum_second(3)
+    sum_last(3)
+    sum_first(0)
+    sum_second(0)
+    sum_last(0)
+
+    @pl.loop(0, BLOCK // 16)
+    def _(i):
+        span = pl.ds(pl.multiple_of(i * 16, 16), 16)
+        total = part[span, :].astype(jnp.float32)
+        for place in (BLOCK, 2 * BLOCK):
+            total += land[pl.ds(pl.multiple_of(place + i * 16, 16), 16), :].astype(jnp.float32)
+        out[span, :] = (hidden[span, :].astype(jnp.float32) + total).astype(jnp.bfloat16)
+
+    for stage in range(5):
+        for kind in range(4):
+            row_copy(stage, kind).wait_send()
+            sum_copy(stage, kind).wait_send()
+        for kind in range(3):
+            meta_copy(stage, kind).wait_send()
+    for k in range(4):
+        lent_copy(k).wait_send()
+        back_copy(k).wait_send()
+
+
+def experts(normed, gates, hidden, w_gate, w_up, w_down):
+    ff = w_gate.shape[2]
+    bf16 = jnp.bfloat16
+    vmem = pl.BlockSpec(memory_space=pltpu.VMEM)
+    hbm = pl.BlockSpec(memory_space=pl.ANY)
+    dma = pltpu.SemaphoreType.DMA
+    return pl.pallas_call(
+        moe_kernel,
+        out_shape=jax.ShapeDtypeStruct((BLOCK, D), bf16),
+        in_specs=[vmem, vmem, vmem, hbm, hbm, hbm],
+        out_specs=vmem,
+        scratch_shapes=[
+            pltpu.VMEM((16 * BLOCK, D), bf16),
+            pltpu.VMEM((16, 32, BLOCK), jnp.float32),
+            pltpu.VMEM((D, ff), bf16),
+            pltpu.VMEM((D, ff), bf16),
+            pltpu.VMEM((ff, D), bf16),
+            pltpu.VMEM((4, 2 * PICK, D), bf16),
+            pltpu.VMEM((4, PICK, D), bf16),
+            pltpu.VMEM((2 * PICK, ff), bf16),
+            pltpu.VMEM((PICK, D), bf16),
+            pltpu.VMEM((4, PICK, D), bf16),
+            pltpu.VMEM((4, PICK, D), bf16),
+            pltpu.VMEM((4, 2 * PICK, WIDE), bf16),
+            pltpu.VMEM((4, 2 * PICK, BLOCK), jnp.float32),
+            pltpu.VMEM((16 * BLOCK, D), bf16),
+            pltpu.VMEM((15 * BLOCK, D), bf16),
+            dma((3,)),
+            dma((20,)),
+            dma((20,)),
+            dma((15,)),
+            dma((15,)),
+            dma((4,)),
+            dma((4,)),
+            dma((4,)),
+            dma((4,)),
+            dma((20,)),
+            dma((20,)),
+        ],
+        compiler_params=pltpu.CompilerParams(
+            collective_id=0, has_side_effects=True, vmem_limit_bytes=60 * 1024 * 1024
+        ),
+        cost_estimate=pl.CostEstimate(
+            flops=2 * 1280 * 3 * D * ff, bytes_accessed=3 * D * ff * 2, transcendentals=1280 * ff
+        ),
+    )(normed, gates, hidden, w_gate, w_up, w_down)
 
 
 def body(
@@ -114,44 +496,13 @@
         * expert_norm[None, :]
     ).astype(jnp.bfloat16)
     logits = jnp.dot(normed, router_weight, preferred_element_type=jnp.float32)
-    score = jax.nn.sigmoid(jnp.take_along_axis(logits, expert_ids, axis=1))
+    experts_all = router_weight.shape[1]
+    chosen = jnp.any(
+        expert_ids[:, :, None] == jnp.arange(experts_all, dtype=jnp.int32)[None, None, :], axis=1
+    )
+    score = jnp.where(chosen, jax.nn.sigmoid(logits), 0.0)
     gates = score / jnp.sum(score, axis=1, keepdims=True)
-    local_experts = w_gate.shape[0]
-    sources = lax.axis_size("ctx")
-    experts_all = local_experts * sources
-    pair_count = row_count * TOPK
-    flat_ids = expert_ids.reshape(pair_count)
-    one_hot = (flat_ids[:, None] == jnp.arange(experts_all, dtype=jnp.int32)[None, :]).astype(
-        jnp.int32
-    )
-    slot_of = jnp.sum((jnp.cumsum(one_hot, axis=0) - one_hot) * one_hot, axis=1)
-    destination = flat_ids * CAP + slot_of
-    repeated = jnp.broadcast_to(normed[:, None, :], (row_count, TOPK, D)).reshape(pair_count, D)
-    outgoing = jnp.zeros((experts_all * CAP, D), jnp.bfloat16).at[destination].set(repeated)
-    outgoing = outgoing.reshape(experts_all, CAP, D)
-    arrived = lax.all_to_all(outgoing, "ctx", split_axis=0, concat_axis=0, tiled=True)
-    slot_count = arrived.shape[1]
-    grouped = arrived.reshape(sources, local_experts, slot_count, D)
-    gate_val = jnp.einsum("sekd,edf->sekf", grouped, w_gate, preferred_element_type=jnp.float32)
-    up_val = jnp.einsum("sekd,edf->sekf", grouped, w_up, preferred_element_type=jnp.float32)
-    activated = (jax.nn.silu(gate_val) * up_val).astype(jnp.bfloat16)
-    produced = jnp.einsum(
-        "sekf,efd->sekd", activated, w_down, preferred_element_type=jnp.float32
-    ).astype(jnp.bfloat16)
-    returned = lax.all_to_all(
-        produced.reshape(sources * local_experts, slot_count, D),
-        "ctx",
-        split_axis=0,
-        concat_axis=0,
-        tiled=True,
-    )
-    picked = (
-        returned.reshape(experts_all * CAP, D)[destination]
-        .astype(jnp.float32)
-        .reshape(row_count, TOPK, D)
-    )
-    expert_sum = jnp.sum(gates[:, :, None] * picked, axis=1)
-    return (hidden_features + expert_sum).astype(jnp.bfloat16)
+    return experts(normed, gates.T, hidden_state, w_gate, w_up, w_down)
 
 
 def solution(mesh):

time: 280 us -> 190 us (0.68)
  Pallas kernels: 0 us -> 120 us
  blocking collectives: 66.6 us -> 0 us
  waiting for transfers between devices: 67.5 us -> 23.3 us
  local copies, waits for them, and re-layouts: 52.4 us -> 11.8 us
  matrix products: 33.6 us -> 7.24 us
  other arithmetic: 31.5 us -> 7.57 us
  starting transfers between devices: 27.1 us -> 19.5 us
    pallas_call x0 -> x1, Pallas kernels: none -> 120 us  [experts(): pl.pallas_call(moe_kernel, out_shape=jax.ShapeDtypeStruct((BLOCK, D), bf1...]
    all_to_all x1 -> x0, blocking collectives: 66.6 us -> none  [body(): lax.all_to_all(outgoing, 'ctx', split_axis=0, concat_axis=0, tiled=True)]
    all_to_all x1 -> x0, waiting for transfers between devices: 56.6 us -> none  [body(): lax.all_to_all(produced.reshape(sources * local_experts, slot_count, D),...]
    dot_general x2 -> x0, matrix products: 21.1 us -> none  [the longest x1 14.7 us: body(): jnp.einsum('sekf,efd->sekd', activated, w_down, preferred_element_type=jn...]
    gather x6 -> x0, local copies, waits for them, and re-layouts: 19.3 us -> none  [the longest x1 12 us: body(): returned.reshape(experts_all * CAP, D)[destination].astype(jnp.float32)]
    all_to_all x1, waiting for transfers between devices: 3.72 us -> 13.9 us  [prefix(): lax.all_to_all(packed, axes, split_axis=0, concat_axis=0, tiled=True)]
    scatter x1 -> x0, local copies, waits for them, and re-layouts: 10.1 us -> none  [body(): jnp.zeros((experts_all * CAP, D), jnp.bfloat16).at[destination]]
    another operation x3 -> x0, other arithmetic: 9.14 us -> none
  transfers between devices with their start and end apart: 4 -> 3, of which waited for: 3 -> 2; matrix products, arithmetic and copies ran while one was open for 11% -> 4% of each run, Pallas kernels for 0% -> 0%
where the time goes in v2:
time: 190 us; the launch traced here: 189 us
  Pallas kernels  120 us (63%)
  waiting for transfers between devices  23.3 us (12%)
  starting transfers between devices  19.5 us (10%)
  local copies, waits for them, and re-layouts  11.8 us (6%)
  other arithmetic  7.57 us (4%)
  matrix products  7.24 us (4%)
    pallas_call x1, Pallas kernels, experts(): pl.pallas_call(moe_kernel, out_shape=jax.ShapeDtypeStruct((BLOCK, D), bf1...  120 us
    all_to_all x1, waiting for transfers between devices, prefix(): lax.all_to_all(packed, axes, split_axis=0, concat_axis=0, tiled=True)  13.9 us
    all_to_all x1, starting transfers between devices, prefix(): lax.all_to_all(packed, axes, split_axis=0, concat_axis=0, tiled=True)  10.6 us
    all_to_all x1, waiting for transfers between devices, prefix(): back = lax.all_to_all(before, axes, split_axis=0, concat_axis=0, tiled=True)  9.41 us
    all_to_all x1, starting transfers between devices, prefix(): back = lax.all_to_all(before, axes, split_axis=0, concat_axis=0, tiled=True)  4.98 us
    unnamed x23, local copies, waits for them, and re-layouts  4.88 us
    ppermute x1, starting transfers between devices, from_behind(): return lax.ppermute(block, axis, route)  3.91 us
  transfers between devices with their start and end apart: 3, of which 2 were waited for; matrix products, arithmetic and copies ran while one was open for 4% of the time, Pallas kernels for 0%

profile of v2, /device:TPU:0, one launch (start us, length us, event | category | flops | bytes accessed | tf_op | source)
XLA Modules:
  0.0 189.4 jit_solution(2873829260909712312)
XLA Ops:
  0.0 0.0 copy-start
  0.0 0.8 slice.47
  0.8 3.9 %collective-permute-start = (bf16[3,2176]{1,0:T(4,128)(2,1)S(1)}, bf16[3,2176]{1,0:T(4,128)(2,1)S(1)}, u32[]{:S(2)}, u32[]{:S(2)}) collective-permute-start(bf16[3,2176]{1,0:T(4,128)(2,1)S(1)} %slice.47), channel_id=1, source_target_pairs={{0,1},{1,2},{2,3},{3,4},{4,5},{5,6},{6,7},{7,8},{8,9},{9,10},{10,1... | collective-permute-start | bytes 39176 | tf_op jit(solution)/shard_map/ppermute | solution.py:23
  4.7 0.7 exp.38
  5.4 0.8 negate_multiply_fusion
  6.2 0.3 reduce_window_sum.11
  6.5 0.2 slice_reduce_fusion.1
  6.7 0.1 exponential_bitcast_fusion
  6.8 1.0 slice_reduce_fusion.5
  7.8 1.4 copy.38
  9.2 0.1 broadcast_in_dim.46
  9.2 0.1 broadcast_in_dim.74
  9.3 0.0 collective-permute-done
  9.3 0.3 copy.37
  9.7 0.0 copy-start.5
  9.7 0.4 maximum_convert_fusion
  10.1 0.3 copy-done.5
  10.4 2.7 %multiply_convert_fusion = bf16[128,2176]{0,1:T(8,128)(2,1)S(1)} fusion(f32[131,2176]{0,1:T(8,128)S(1)} %maximum_convert_fusion, f32[2176]{0:T(1024)S(1)} %get-tuple-element.7, f32[2176]{0:T(1024)S(1)} %get-tuple-element.8, f32[2176]{0:T(1024)S(1)} %get-tuple-element.6, f32[2176]{0:T(1024)S(1)} %get-tuple-element.5, f32[2176]{0:T(1024)S(1)} %copy-done.5), kind=kLoop, calls=%fused_computation.30 | loop fusion | flops 3620864 | bytes 5057024 | tf_op jit(solution)/shard_map/convert_element_type | solution.py:470
  13.2 0.6 fusion.22
  13.8 0.3 reshape.66
  14.1 0.1 broadcast_in_dim.75
  14.2 0.1 pad_maximum_fusion
  14.3 0.0 copy-start.8
  14.3 1.2 all_to_all.14
  15.5 10.6 %all-to-all-start = ((f32[128,1,1152]{2,1,0:T(1,128)}), f32[128,1,1152]{2,1,0:T(1,128)S(1)}, u32[]{:S(2)}, u32[]{:S(2)}) async-start(f32[128,1,1152]{2,1,0:T(1,128)} %all_to_all.14), calls=%async_computation | async-start | bytes 1179648 | tf_op jit(solution)/shard_map/all_to_all | solution.py:34
  26.1 0.0 copy-done.8
  26.2 13.9 %all-to-all-done = f32[128,1,1152]{2,1,0:T(1,128)S(1)} async-done(((f32[128,1,1152]{2,1,0:T(1,128)}), f32[128,1,1152]{2,1,0:T(1,128)S(1)}, u32[]{:S(2)}, u32[]{:S(2)}) %all-to-all-start) | async-done | bytes 589856 | tf_op jit(solution)/shard_map/all_to_all | solution.py:34
  40.1 0.1 slice_reduce_fusion
  40.2 0.2 fusion.13
  40.4 0.6 convolution_bitcast_fusion
  41.0 1.3 copy.39
  42.3 5.0 %all-to-all-start.1 = ((f32[128,1,1024]{2,1,0:T(1,128)}), f32[128,1,1024]{2,1,0:T(1,128)S(1)}, u32[]{:S(2)}, u32[]{:S(2)}) async-start(f32[128,1,1024]{2,1,0:T(1,128)} %copy.39), calls=%async_computation.1 | async-start | bytes 1048576 | tf_op jit(solution)/shard_map/all_to_all | solution.py:43
  47.3 0.2 fusion.45
  47.5 3.4 %fusion.7 = f32[128,32,64]{0,2,1:T(8,128)} fusion(bf16[128,32,64]{0,2,1:T(8,128)(2,1)S(1)} %bitcast.27, f32[32,128]{1,0:T(8,128)S(1)} %get-tuple-element.12, f32[128,128]{1,0:T(8,128)S(1)} %fusion.45, f32[32,128]{1,0:T(8,128)S(1)} %reduce_window_sum.11, pred[128,128]{1,0:T(8,128)(4,1)S(1)} %iota_compare_fusion.2), kind=kOutput, calls=%fused_computation.7 | convolution fusion | flops 405274624 | bytes 1687552 | tf_op jit(solution)/shard_map/hts,shp->thp/dot_general | solution.py:57
  51.0 0.0 copy-start.9
  51.0 9.4 %all-to-all-done.1 = f32[128,1,1024]{2,1,0:T(1,128)S(1)} async-done(((f32[128,1,1024]{2,1,0:T(1,128)}), f32[128,1,1024]{2,1,0:T(1,128)S(1)}, u32[]{:S(2)}, u32[]{:S(2)}) %all-to-all-start.1) | async-done | bytes 524320 | tf_op jit(solution)/shard_map/all_to_all | solution.py:43
  60.4 1.2 reduce.6
  61.6 0.3 reshape.67
  61.9 0.0 copy-done.9
  61.9 1.9 fusion.11
  63.8 0.0 copy-start.1
  63.8 0.3 copy.40
  64.2 0.7 copy-done.1
  64.9 0.0 copy-start.4
  64.9 0.0 copy-start.6
  64.9 0.4 multiply_reduce_fusion
  65.3 0.6 copy-done.4
  65.9 0.0 copy-done.6
  65.9 0.0 copy-start.7
  65.9 0.6 fusion.27
  66.5 0.0 copy-start.2
  66.6 0.0 copy-done.7
  66.6 0.2 fusion.29.normed
  66.8 0.0 copy-done
  66.8 0.0 copy-start.3
  66.8 0.3 fusion.51
  67.1 0.6 divide_bitcast_fusion.gates
  67.7 0.0 copy-done.2
  67.7 0.0 copy-done.3
  67.7 119.7 %shard_map.154 = bf16[128,2048]{1,0:T(8,128)(2,1)} custom-call(bf16[128,2048]{1,0:T(8,128)(2,1)} %copy-done.3, f32[32,128]{1,0:T(8,128)} %divide_bitcast_fusion.gates, bf16[128,2048]{1,0:T(8,128)(2,1)} %copy-done.2, bf16[1,2048,768]{2,1,0:T(8,128)(2,1)} %w_gate.1, bf16[1,2048,768]{2,1,0:T(8,128)(2,1)} %w_up.1, bf16[1,768,2048]{2,1,0:T(8,128)(2,1)} %w_down.1), custom_call_target="tpu_custom_call" | custom-call | flops 12079595520 | bytes 9437184 | tf_op jit(solution)/shard_map/pallas_call | solution.py:404
  187.5 1.9 copy.45
  (6 shorter events, 0.1 us)
Async XLA Ops:
  0.0 66.8 %copy-start = (bf16[2048,32]{0,1:T(8,128)(2,1)S(1)}, bf16[2048,32]{0,1:T(8,128)(2,1)}, u32[]{:S(2)}) copy-start(bf16[2048,32]{0,1:T(8,128)(2,1)} %param.27) | copy-start | bytes 393220
  0.8 8.5 %collective-permute-start = (bf16[3,2176]{1,0:T(4,128)(2,1)S(1)}, bf16[3,2176]{1,0:T(4,128)(2,1)S(1)}, u32[]{:S(2)}, u32[]{:S(2)}) collective-permute-start(bf16[3,2176]{1,0:T(4,128)(2,1)S(1)} %slice.47), channel_id=1, source_target_pairs={{0,1},{1,2},{2,3},{3,4},{4,5},{5,6},{6,7},{7,8},{8,9},{9,10},{10,1... | collective-permute-start | bytes 39176 | tf_op jit(solution)/shard_map/ppermute | solution.py:23
  9.7 0.7 copy-start.5
  14.3 11.8 %copy-start.8 = (s32[128,8]{0,1:T(8,128)S(1)}, s32[128,8]{0,1:T(8,128)}, u32[]{:S(2)}) copy-start(s32[128,8]{0,1:T(8,128)} %param.28) | copy-start | bytes 12292
  15.5 24.5 %all-to-all-start = ((f32[128,1,1152]{2,1,0:T(1,128)}), f32[128,1,1152]{2,1,0:T(1,128)S(1)}, u32[]{:S(2)}, u32[]{:S(2)}) async-start(f32[128,1,1152]{2,1,0:T(1,128)} %all_to_all.14), calls=%async_computation | async-start | bytes 1179648 | tf_op jit(solution)/shard_map/all_to_all | solution.py:34
  42.3 18.0 %all-to-all-start.1 = ((f32[128,1,1024]{2,1,0:T(1,128)}), f32[128,1,1024]{2,1,0:T(1,128)S(1)}, u32[]{:S(2)}, u32[]{:S(2)}) async-start(f32[128,1,1024]{2,1,0:T(1,128)} %copy.39), calls=%async_computation.1 | async-start | bytes 1048576 | tf_op jit(solution)/shard_map/all_to_all | solution.py:43
  51.0 10.9 %copy-start.9 = (f32[32]{0:T(128)S(1)}, f32[32]{0:T(128)}, u32[]{:S(2)}) copy-start(f32[32]{0:T(128)} %param.23) | copy-start | bytes 388
  63.8 1.0 copy-start.1
  64.9 1.0 copy-start.4
  64.9 1.0 copy-start.6
  65.9 0.7 copy-start.7
  66.5 1.2 copy-start.2
  66.8 0.9 copy-start.3

commit v3 on v2

--- a/solution.py
+++ b/solution.py
@@ -12,55 +12,10 @@
 KERNEL = 4
 TOPK = 8
 CAP = 40
+CONV = 2176
 
 
 EXACT = lax.Precision.HIGHEST
-
-
-def from_behind(block, axis, distance):
-    devices = range(lax.axis_size(axis))
-    route = [(i - distance, i) for i in devices if i - distance in devices]
-    return lax.ppermute(block, axis, route)
-
-
-def prefix(state_local, log_through):
-    axes = ("ctx", "exp")
-    devices = lax.axis_size(axes)
-    share = HEADS * HEAD_DIM * STATE // devices
-    per_head = devices // HEADS
-    pieces = state_local.reshape(devices, share)
-    logs = jnp.repeat(log_through, per_head)[:, None]
-    packed = jnp.concatenate([pieces, jnp.broadcast_to(logs, (devices, 128))], axis=1)
-    arrived = lax.all_to_all(packed, axes, split_axis=0, concat_axis=0, tiled=True)
-    states, log = arrived[:, :share], arrived[:, share]
-    place = jnp.arange(devices)
-    lower = place[:, None] > place[None, :]
-    gap = jnp.dot(
-        jnp.where(lower, log[None, :], 0.0), lower.astype(jnp.float32), precision=EXACT
-    )
-    weight = jnp.where(lower, jnp.exp(jnp.minimum(gap, 0.0)), 0.0)
-    before = jnp.dot(weight, states, precision=EXACT)
-    back = lax.all_to_all(before, axes, split_axis=0, concat_axis=0, tiled=True)
-    return back.reshape(HEADS, HEAD_DIM, STATE)
-
-
-def block_terms(x_block, input_map, output_map, increment_tile, decay_rate):
-    count = x_block.shape[0]
-    cum_log = jnp.cumsum(-increment_tile * decay_rate[:, None], axis=1)
-    capacity_cells = jnp.arange(count)
-    causal = capacity_cells[:, None] >= capacity_cells[None, :]
-    gap_log = jnp.where(causal[None], cum_log[:, :, None] - cum_log[:, None, :], 0.0)
-    inside_offset = jnp.where(causal[None], jnp.exp(gap_log), 0.0)
-    cross_gram = jnp.dot(output_map, input_map.T, preferred_element_type=jnp.float32)
-    mixing = inside_offset * cross_gram[None] * increment_tile[:, None, :]
-    head_view = x_block.astype(jnp.float32).reshape(count, HEADS, HEAD_DIM)
-    inner_y = jnp.einsum("hts,shp->thp", mixing, head_view, precision=EXACT)
-    tail_w = jnp.exp(cum_log[:, -1:] - cum_log) * increment_tile
-    weighted = head_view * tail_w.T[:, :, None]
-    state_local = jnp.einsum(
-        "shp,sn->hpn", weighted, input_map.astype(jnp.float32), precision=EXACT
-    )
-    return (inner_y, jnp.exp(cum_log), state_local, cum_log[:, -1], head_view)
 
 
 MESH = pl.DeviceIdType.MESH
@@ -443,6 +398,406 @@
     )(normed, gates, hidden, w_gate, w_up, w_down)
 
 
+COLUMN = 8
+TILE = D // COLUMN
+FLAT = 16
+
+
+def sigmoid(value):
+    return 1.0 / (1.0 + jnp.exp(-value))
+
+
+def split(value, count):
+    pieces = []
+    for _ in range(count):
+        piece = value.astype(jnp.bfloat16)
+        pieces.append(piece)
+        value = value - piece.astype(jnp.float32)
+    return jnp.concatenate(pieces, axis=1)
+
+
+def mixer_kernel(
+    entry,
+    gate,
+    residual,
+    step,
+    step_bias,
+    decay_log,
+    taps,
+    tap_bias,
+    skip,
+    mixer_gain,
+    expert_norm,
+    router,
+    ids,
+    normed,
+    hidden,
+    gates,
+    padded,
+    mixed,
+    cum,
+    delta,
+    cum_cols,
+    tail_cols,
+    entry_cols,
+    last_cols,
+    gram,
+    piece,
+    first,
+    earlier,
+    earlier_log,
+    total,
+    second,
+    third,
+    state,
+    inner,
+    value,
+    halo_send,
+    halo_recv,
+    first_send,
+    first_recv,
+    second_send,
+    second_recv,
+    third_send,
+    third_recv,
+):
+    ctx = lax.axis_index("ctx")
+    depth = lax.axis_index("exp")
+    core = ctx % 2
+    column = ctx // 2
+    me = core * 4 + depth
+    f32, bf16 = jnp.float32, jnp.bfloat16
+
+    def member(m):
+        return (column * 2 + m // 4, m % 4)
+
+    def peer(c):
+        return (c * 2 + core, depth)
+
+    last = (me == COLUMN - 1).astype(jnp.int32)
+    after = (((column + last) % FLAT) * 2 + ((me + 1) % COLUMN) // 4, (me + 1) % 4)
+    initial = (me == 0).astype(jnp.int32)
+    ahead = (
+        ((column - initial + FLAT) % FLAT) * 2 + ((me + COLUMN - 1) % COLUMN) // 4,
+        (me + COLUMN - 1) % 4,
+    )
+
+    barrier = pltpu.get_barrier_semaphore()
+    for i in range(1, COLUMN):
+        pl.semaphore_signal(
+            barrier, inc=1, device_id=member((me + i) % COLUMN), device_id_type=MESH
+        )
+    for i in range(1, FLAT):
+        pl.semaphore_signal(
+            barrier, inc=1, device_id=peer((column + i) % FLAT), device_id_type=MESH
+        )
+
+    @pl.when(me == COLUMN - 1)
+    def _():
+        pl.semaphore_signal(barrier, inc=1, device_id=after, device_id_type=MESH)
+
+    @pl.when(me == 0)
+    def _():
+        pl.semaphore_signal(barrier, inc=1, device_id=ahead, device_id_type=MESH)
+
+    padded[16:, :] = entry[...]
+    pl.semaphore_wait(barrier, COLUMN + FLAT - 2 + last + initial)
+
+    def remote(src, dst, send, recv, to):
+        return pltpu.make_async_remote_copy(
+            src_ref=src, dst_ref=dst, send_sem=send, recv_sem=recv, device_id=to, device_id_type=MESH
+        )
+
+    halo = remote(
+        entry.at[pl.ds(BLOCK - 16, 16)], padded.at[pl.ds(0, 16)], halo_send.at[0], halo_recv.at[0], after
+    )
+    halo.start()
+
+    row_id = lax.broadcasted_iota(jnp.int32, (BLOCK, BLOCK), 0)
+    lane_id = lax.broadcasted_iota(jnp.int32, (BLOCK, BLOCK), 1)
+    shifted = step[...] + step_bias[...]
+    width = jnp.maximum(shifted, 0.0) + jnp.log1p(jnp.exp(-jnp.abs(shifted)))
+    logs = -width * jnp.exp(decay_log[...])
+    summed = jnp.dot(
+        logs, (row_id <= lane_id).astype(f32), precision=EXACT, preferred_element_type=f32
+    )
+    cum[...] = summed
+    delta[...] = width
+
+    def upright(a):
+        return jnp.concatenate([a, jnp.zeros((BLOCK - HEADS, BLOCK), f32)], axis=0).T[:, :HEADS]
+
+    summed_t = upright(summed)
+    width_t = upright(width)
+    final = summed_t[BLOCK - 1 :, :]
+    cum_cols[...] = split(summed_t, 3)
+    tail_cols[...] = split(jnp.exp(final - summed_t) * width_t, 2)
+    entry_cols[...] = split(jnp.exp(summed_t), 2)
+    last_cols[...] = split(jnp.broadcast_to(final, (16, HEADS)), 3)
+
+    def spread(m, copies, per, count):
+        head = lax.broadcasted_iota(jnp.int32, (HEADS, count), 0)
+        lane = lax.broadcasted_iota(jnp.int32, (HEADS, count), 1)
+        one = (head == 4 * m + lane // per).astype(bf16)
+        return jnp.concatenate([one] * copies, axis=0)
+
+    halo.wait_recv()
+    keep = (ctx + depth > 0).astype(f32)
+
+    @pl.loop(0, CONV // 128)
+    def _(n):
+        cols = pl.ds(pl.multiple_of(n * 128, 128), 128)
+        full = jnp.concatenate(
+            [padded[0:16, cols].astype(f32) * keep, padded[16:, cols].astype(f32)], axis=0
+        )
+        acc = jnp.broadcast_to(tap_bias[:, cols], (BLOCK, 128))
+        for j in range(KERNEL):
+            acc = acc + taps[j : j + 1, cols] * full[13 + j : 13 + j + BLOCK]
+        mixed[:, cols] = (acc * sigmoid(acc)).astype(bf16)
+
+    in_map = mixed[:, D : D + STATE]
+    out_map = mixed[:, D + STATE : D + 2 * STATE]
+    cross = lax.dot_general(
+        out_map, in_map, (((1,), (1,)), ((), ())), preferred_element_type=f32
+    )
+    gram[...] = jnp.where(row_id >= lane_id, cross, 0.0)
+    in_twice = jnp.concatenate([in_map, in_map], axis=0)
+
+    def first_copy(m, slot):
+        return remote(piece.at[m], first.at[slot], first_send.at[m], first_recv.at[slot], member(m))
+
+    @pl.loop(0, COLUMN)
+    def _(i):
+        m = (me + 1 + i) % COLUMN
+        cols = pl.ds(pl.multiple_of(m * TILE, TILE), TILE)
+        weight = jnp.dot(tail_cols[...], spread(m, 2, HEAD_DIM, TILE), preferred_element_type=f32)
+        weighted = mixed[:, cols].astype(f32) * weight
+        high = weighted.astype(bf16)
+        low = (weighted - high.astype(f32)).astype(bf16)
+        piece[m, 0:STATE, :] = lax.dot_general(
+            in_twice,
+            jnp.concatenate([high, low], axis=0),
+            (((0,), (0,)), ((), ())),
+            preferred_element_type=f32,
+        )
+        ends = jnp.dot(last_cols[...], spread(m, 3, HEAD_DIM, TILE), preferred_element_type=f32)
+        piece[m, STATE : STATE + 8, :] = ends[0:8]
+
+        @pl.when(i < COLUMN - 1)
+        def _():
+            first_copy(m, me).start()
+
+    first[me] = piece[me]
+
+    @pl.loop(0, COLUMN)
+    def _(m):
+        @pl.when(m != me)
+        def _():
+            first_copy(m, m).wait_recv()
+
+    run = jnp.zeros((STATE, TILE), f32)
+    run_log = jnp.zeros((8, TILE), f32)
+    for m in range(COLUMN):
+        earlier[m] = run
+        earlier_log[m] = run_log
+        log = first[m, STATE : STATE + 8, :]
+        run = run * jnp.exp(log[0:1]) + first[m, 0:STATE, :]
+        run_log = run_log + log
+    total[0:STATE, :] = run
+    total[STATE : STATE + 8, :] = run_log
+
+    def second_copy(o):
+        return remote(
+            total, second.at[o], second_send.at[o], second_recv.at[o], peer((column + o) % FLAT)
+        )
+
+    @pl.loop(1, FLAT)
+    def _(o):
+        @pl.when(column + o < FLAT)
+        def _():
+            second_copy(o).start()
+
+    @pl.loop(0, COLUMN)
+    def _(m):
+        cols = pl.ds(pl.multiple_of(m * TILE, TILE), TILE)
+        upto = jnp.dot(cum_cols[...], spread(m, 3, BLOCK, 4 * BLOCK), preferred_element_type=f32)
+        feature = mixed[:, cols]
+        lane = lax.broadcasted_iota(jnp.int32, (BLOCK, TILE), 1) // HEAD_DIM
+        highs, lows, blocks = [], [], []
+        for j in range(4):
+            head = pl.ds(4 * m + j, 1)
+            gap = upto[:, BLOCK * j : BLOCK * (j + 1)] - cum[head, :]
+            mix = jnp.exp(jnp.minimum(gap, 0.0)) * gram[...] * delta[head, :]
+            mix = mix + jnp.where(row_id == lane_id, skip[4 * m + j], 0.0)
+            high = mix.astype(bf16)
+            highs.append(high)
+            lows.append((mix - high.astype(f32)).astype(bf16))
+            blocks.append(jnp.where(lane == j, feature, jnp.zeros_like(feature)))
+        diagonal = jnp.concatenate(blocks, axis=0)
+        inner[:, cols] = jnp.dot(
+            jnp.concatenate(highs, axis=1), diagonal, preferred_element_type=f32
+        ) + jnp.dot(jnp.concatenate(lows, axis=1), diagonal, preferred_element_type=f32)
+
+    value[0:STATE, 0:TILE] = jnp.zeros((STATE, TILE), f32)
+
+    @pl.loop(1, FLAT)
+    def _(i):
+        o = FLAT - i
+
+        @pl.when(o <= column)
+        def _():
+            second_copy(o).wait_recv()
+            value[0:STATE, 0:TILE] = (
+                value[0:STATE, 0:TILE] * jnp.exp(second[o, STATE : STATE + 1, :])
+                + second[o, 0:STATE, :]
+            )
+
+    def third_copy(m, slot):
+        return remote(third.at[m], state.at[slot], third_send.at[m], third_recv.at[slot], member(m))
+
+    @pl.loop(0, COLUMN)
+    def _(i):
+        m = (me + 1 + i) % COLUMN
+        third[m] = (
+            value[0:STATE, 0:TILE] * jnp.exp(earlier_log[m, 0:1, :]) + earlier[m]
+        ).astype(bf16)
+
+        @pl.when(i < COLUMN - 1)
+        def _():
+            third_copy(m, me).start()
+
+    state[me] = third[me]
+
+    @pl.loop(0, COLUMN)
+    def _(m):
+        @pl.when(m != me)
+        def _():
+            third_copy(m, m).wait_recv()
+
+    def fold(a):
+        return a[:, :128] + a[:, 128:]
+
+    def carry(m, square):
+        cols = pl.ds(pl.multiple_of(m * TILE, TILE), TILE)
+        carried = jnp.dot(out_map, state[m], preferred_element_type=f32)
+        weight = jnp.dot(entry_cols[...], spread(m, 2, HEAD_DIM, TILE), preferred_element_type=f32)
+        branch = gate[:, cols].astype(f32)
+        v = (inner[:, cols] + carried * weight) * (branch * sigmoid(branch))
+        value[:, cols] = v
+        return square + fold(v * v)
+
+    zero = jnp.zeros((BLOCK, 128), f32)
+    square = lax.fori_loop(0, COLUMN, carry, zero)
+    scale = lax.rsqrt(jnp.sum(square, axis=1, keepdims=True) * (1.0 / D) + 1e-05)
+
+    def join(m, square):
+        cols = pl.ds(pl.multiple_of(m * TILE, TILE), TILE)
+        out = value[:, cols] * scale * mixer_gain[:, cols]
+        kept = (residual[:, cols].astype(f32) + out).astype(bf16)
+        hidden[:, cols] = kept
+        wide = kept.astype(f32)
+        return square + fold(wide * wide)
+
+    square = lax.fori_loop(0, COLUMN, join, zero)
+    again = lax.rsqrt(jnp.sum(square, axis=1, keepdims=True) * (1.0 / D) + 1e-05)
+
+    @pl.loop(0, COLUMN)
+    def _(m):
+        cols = pl.ds(pl.multiple_of(m * TILE, TILE), TILE)
+        normed[:, cols] = (hidden[:, cols].astype(f32) * again * expert_norm[:, cols]).astype(bf16)
+
+    logits = lax.dot_general(
+        router[...], normed[...], (((1,), (1,)), ((), ())), preferred_element_type=f32
+    )
+    expert = lax.broadcasted_iota(jnp.int32, (32, BLOCK), 0)
+    chosen = expert < 0
+    for k in range(TOPK):
+        chosen = chosen | (expert == ids[k : k + 1, :])
+    score = jnp.where(chosen, sigmoid(logits), 0.0)
+    gates[...] = score / jnp.sum(score, axis=0, keepdims=True)
+
+    halo.wait_send()
+
+    @pl.loop(0, COLUMN)
+    def _(m):
+        @pl.when(m != me)
+        def _():
+            first_copy(m, me).wait_send()
+            third_copy(m, me).wait_send()
+
+    @pl.loop(1, FLAT)
+    def _(o):
+        @pl.when(column + o < FLAT)
+        def _():
+            second_copy(o).wait_send()
+
+
+def mixer(entry, gate, residual, step, bias, decay_log, taps, tap_bias, skip, gain, norm, router, ids):
+    f32, bf16 = jnp.float32, jnp.bfloat16
+    vmem = pl.BlockSpec(memory_space=pltpu.VMEM)
+    smem = pl.BlockSpec(memory_space=pltpu.SMEM)
+    dma = pltpu.SemaphoreType.DMA
+    return pl.pallas_call(
+        mixer_kernel,
+        out_shape=(
+            jax.ShapeDtypeStruct((BLOCK, D), bf16),
+            jax.ShapeDtypeStruct((BLOCK, D), bf16),
+            jax.ShapeDtypeStruct((32, BLOCK), f32),
+        ),
+        in_specs=[vmem] * 8 + [smem] + [vmem] * 4,
+        out_specs=(vmem, vmem, vmem),
+        scratch_shapes=[
+            pltpu.VMEM((BLOCK + 16, CONV), bf16),
+            pltpu.VMEM((BLOCK, CONV), bf16),
+            pltpu.VMEM((HEADS, BLOCK), f32),
+            pltpu.VMEM((HEADS, BLOCK), f32),
+            pltpu.VMEM((BLOCK, 3 * HEADS), bf16),
+            pltpu.VMEM((BLOCK, 2 * HEADS), bf16),
+            pltpu.VMEM((BLOCK, 2 * HEADS), bf16),
+            pltpu.VMEM((16, 3 * HEADS), bf16),
+            pltpu.VMEM((BLOCK, BLOCK), f32),
+            pltpu.VMEM((COLUMN, STATE + 8, TILE), f32),
+            pltpu.VMEM((COLUMN, STATE + 8, TILE), f32),
+            pltpu.VMEM((COLUMN, STATE, TILE), f32),
+            pltpu.VMEM((COLUMN, 8, TILE), f32),
+            pltpu.VMEM((STATE + 8, TILE), f32),
+            pltpu.VMEM((FLAT, STATE + 8, TILE), f32),
+            pltpu.VMEM((COLUMN, STATE, TILE), bf16),
+            pltpu.VMEM((COLUMN, STATE, TILE), bf16),
+            pltpu.VMEM((BLOCK, D), f32),
+            pltpu.VMEM((BLOCK, D), f32),
+            dma((1,)),
+            dma((1,)),
+            dma((COLUMN,)),
+            dma((COLUMN,)),
+            dma((FLAT,)),
+            dma((FLAT,)),
+            dma((COLUMN,)),
+            dma((COLUMN,)),
+        ],
+        compiler_params=pltpu.CompilerParams(
+            collective_id=1, has_side_effects=True, vmem_limit_bytes=48 * 1024 * 1024
+        ),
+        cost_estimate=pl.CostEstimate(
+            flops=2 * BLOCK * 512 * D * 3, bytes_accessed=BLOCK * D * 12, transcendentals=BLOCK * D * 5
+        ),
+    )(
+        entry,
+        gate,
+        residual,
+        step,
+        bias[:, None],
+        decay_log[:, None],
+        taps,
+        tap_bias[None, :],
+        skip,
+        gain[None, :],
+        norm[None, :],
+        router.T,
+        ids.T,
+    )
+
+
 def body(
     filter_entry_array,
     gate_input,
@@ -461,48 +816,22 @@
     w_up,
     w_down,
 ):
-    row_count = filter_entry_array.shape[0]
-    rim_rows = from_behind(filter_entry_array[row_count - (KERNEL - 1) :], ("ctx", "exp"), 1)
-    padded = jnp.concatenate([rim_rows, filter_entry_array], axis=0).astype(jnp.float32)
-    summed = jnp.zeros((row_count, padded.shape[1]), jnp.float32) + conv_bias[None, :]
-    for offset in range(KERNEL):
-        summed = summed + conv_weight[offset][None, :] * padded[offset : offset + row_count]
-    filter_result_array = jax.nn.silu(summed).astype(jnp.bfloat16)
-    x_block = filter_result_array[:, :D]
-    input_map = filter_result_array[:, D : D + STATE]
-    output_map = filter_result_array[:, D + STATE :]
-    step_size = jax.nn.softplus(step_unshifted + step_bias[:, None])
-    decay_rate = jnp.exp(decay_log)
-    inner_y, entry_w, state_local, through, head_view = block_terms(
-        x_block, input_map, output_map, step_size, decay_rate
+    normed, hidden, gates = mixer(
+        filter_entry_array,
+        gate_input,
+        residual,
+        step_unshifted,
+        step_bias,
+        decay_log,
+        conv_weight,
+        conv_bias,
+        skip_gain,
+        mixer_gain,
+        expert_norm,
+        router_weight,
+        expert_ids,
     )
-    before = prefix(state_local, through)
-    carried = entry_w.T[:, :, None] * jnp.einsum(
-        "tn,hpn->thp", output_map.astype(jnp.float32), before, precision=EXACT
-    )
-    direct = skip_gain[None, :, None] * head_view
-    ssm_out = (inner_y + carried + direct).reshape(row_count, D)
-    gated = ssm_out * jax.nn.silu(gate_input.astype(jnp.float32))
-    mixer_out = (
-        gated
-        * lax.rsqrt(jnp.mean(gated * gated, axis=-1, keepdims=True) + 1e-05)
-        * mixer_gain[None, :]
-    )
-    hidden_state = (residual.astype(jnp.float32) + mixer_out).astype(jnp.bfloat16)
-    hidden_features = hidden_state.astype(jnp.float32)
-    normed = (
-        hidden_features
-        * lax.rsqrt(jnp.mean(hidden_features * hidden_features, axis=-1, keepdims=True) + 1e-05)
-        * expert_norm[None, :]
-    ).astype(jnp.bfloat16)
-    logits = jnp.dot(normed, router_weight, preferred_element_type=jnp.float32)
-    experts_all = router_weight.shape[1]
-    chosen = jnp.any(
-        expert_ids[:, :, None] == jnp.arange(experts_all, dtype=jnp.int32)[None, None, :], axis=1
-    )
-    score = jnp.where(chosen, jax.nn.sigmoid(logits), 0.0)
-    gates = score / jnp.sum(score, axis=1, keepdims=True)
-    return experts(normed, gates.T, hidden_state, w_gate, w_up, w_down)
+    return experts(normed, gates, hidden, w_gate, w_up, w_down)
 
 
 def solution(mesh):

time: 190 us -> 185 us (0.974)
  Pallas kernels: 120 us -> 170 us
  waiting for transfers between devices: 23.3 us -> 0 us
  starting transfers between devices: 19.5 us -> 0 us
  other arithmetic: 7.57 us -> 0 us
  matrix products: 7.24 us -> 0 us
  local copies, waits for them, and re-layouts: 11.8 us -> 14.5 us
    pallas_call x0 -> x1, Pallas kernels: none -> 36.2 us  [mixer(): pl.pallas_call(mixer_kernel, out_shape=(jax.ShapeDtypeStruct((BLOCK, D),...]
    all_to_all x2 -> x0, waiting for transfers between devices: 23.3 us -> none  [the longest x1 13.9 us: prefix(): lax.all_to_all(packed, axes, split_axis=0, concat_axis=0, tiled=True)]
    all_to_all x2 -> x0, starting transfers between devices: 15.6 us -> none  [the longest x1 10.6 us: prefix(): lax.all_to_all(packed, axes, split_axis=0, concat_axis=0, tiled=True)]
    pallas_call x1, Pallas kernels: 120 us -> 134 us  [experts(): pl.pallas_call(moe_kernel, out_shape=jax.ShapeDtypeStruct((BLOCK, D), bf1...]
    unnamed x23 -> x27, local copies, waits for them, and re-layouts: 4.88 us -> 12.3 us
    dot_general x7 -> x0, matrix products: 7.24 us -> none  [the longest x1 3.43 us: block_terms(): inner_y = jnp.einsum('hts,shp->thp', mixing, head_view, precision=EXACT)]
    ppermute x1 -> x0, starting transfers between devices: 3.91 us -> none  [from_behind(): return lax.ppermute(block, axis, route)]
    convert_element_type x3 -> x0, other arithmetic: 3.37 us -> none  [the longest x1 2.74 us: body(): filter_result_array = jax.nn.silu(summed).astype(jnp.bfloat16)]
  transfers between devices with their start and end apart: 3 -> 0, of which waited for: 2 -> 0; matrix products, arithmetic and copies ran while one was open for 4% -> 0% of each run, Pallas kernels for 0% -> 0%
where the time goes in v3:
time: 185 us; the launch traced here: 184 us
  Pallas kernels  170 us (92%)
  local copies, waits for them, and re-layouts  14.5 us (8%)
    pallas_call x1, Pallas kernels, experts(): pl.pallas_call(moe_kernel, out_shape=jax.ShapeDtypeStruct((BLOCK, D), bf1...  134 us
    pallas_call x1, Pallas kernels, mixer(): pl.pallas_call(mixer_kernel, out_shape=(jax.ShapeDtypeStruct((BLOCK, D),...  36.2 us
    unnamed x27, local copies, waits for them, and re-layouts  12.3 us

profile of v3, /device:TPU:0, one launch (start us, length us, event | category | flops | bytes accessed | tf_op | source)
XLA Modules:
  0.0 184.4 jit_solution(5365896470879574237)
XLA Ops:
  0.0 0.7 broadcast_in_dim.17.tap_bias
  0.7 0.7 copy.17.step_bias
  1.4 0.7 copy.18.decay_log
  2.2 0.0 copy-start
  2.2 1.1 copy-done
  3.2 0.0 copy-start.1
  3.2 1.0 copy-done.1
  4.3 0.0 copy-start.2
  4.3 1.0 copy-done.2
  5.3 0.0 copy-start.3
  5.3 0.9 copy-done.3
  6.2 0.0 copy-start.4
  6.2 0.8 copy-done.4
  7.0 0.0 copy-start.5
  7.0 0.7 copy-done.5
  7.7 0.0 copy-start.6
  7.7 0.7 copy-done.6
  8.4 0.0 copy-start.7
  8.4 0.7 copy-done.7
  9.1 0.0 copy-start.8
  9.1 0.7 copy-done.8
  9.8 0.0 copy-start.9
  9.8 0.7 copy-done.9
  10.4 36.2 %shard_map.154 = (bf16[128,2048]{1,0:T(8,128)(2,1)S(1)}, bf16[128,2048]{1,0:T(8,128)(2,1)S(1)}, f32[32,128]{1,0:T(8,128)S(1)}) custom-call(bf16[128,2176]{1,0:T(8,128)(2,1)S(1)} %copy-done, bf16[128,2048]{1,0:T(8,128)(2,1)S(1)} %copy-done.1, bf16[128,2048]{1,0:T(8,128)(2,1)S(1)} %copy-done.2, f32[32,128]{1,0:T(8,128)S(1)} %copy-done.5, ...), custom_call_target="tpu_custom_call" | custom-call | flops 805306368 | bytes 3145728 | tf_op jit(solution)/shard_map/pallas_call | solution.py:740
  46.6 0.0 copy-start.10
  46.6 0.8 copy-done.10
  47.4 0.0 copy-start.11
  47.4 0.8 copy-done.11
  48.2 0.0 copy-start.12
  48.2 0.6 copy-done.12
  48.8 133.7 %shard_map.155 = bf16[128,2048]{1,0:T(8,128)(2,1)} custom-call(bf16[128,2048]{1,0:T(8,128)(2,1)} %copy-done.10, f32[32,128]{1,0:T(8,128)} %copy-done.12, bf16[128,2048]{1,0:T(8,128)(2,1)} %copy-done.11, bf16[1,2048,768]{2,1,0:T(8,128)(2,1)} %w_gate.1, bf16[1,2048,768]{2,1,0:T(8,128)(2,1)} %w_up.1, bf16[1,768,2048]{2,1,0:T(8,128)(2,1)} %w_down.1), custom_call_target="tpu_custom_call" | custom-call | flops 12079595520 | bytes 9437184 | tf_op jit(solution)/shard_map/pallas_call | solution.py:359
  182.5 1.9 %copy.20 = bf16[128,2048]{1,0:T(8,128)(2,1)} copy(bf16[128,2048]{1,0:T(8,128)(2,1)} %shard_map.155) | data formatting | bytes 1048576
Async XLA Ops:
  2.2 1.1 copy-start
  3.2 1.0 copy-start.1
  4.3 1.0 copy-start.2
  5.3 0.9 copy-start.3
  6.2 0.8 copy-start.4
  7.0 0.7 copy-start.5
  7.7 0.7 copy-start.6
  8.4 0.7 copy-start.7
  9.1 0.7 copy-start.8
  9.8 0.7 copy-start.9
  46.6 0.8 copy-start.10
  47.4 0.8 copy-start.11
  48.2 0.6 copy-start.12

commit v4 on v0

v4 whole, which is shorter than its diff:
```python
import types

import jax
import jax.numpy as jnp
from jax import lax
from jax.experimental import pallas as pl
from jax.experimental.pallas import tpu as pltpu
from jax.sharding import PartitionSpec as P

D = 2048
HEADS = 32
HEAD_DIM = 64
STATE = 64
KERNEL = 4
TOPK = 8
CAP = 40
CONV = 2176
FF = 768
EXPERTS = 32
BLOCK = 128
HALF = BLOCK // 2
PICK = 4 * CAP
WIDE = 4 * BLOCK
COLUMN = 8
TILE = D // COLUMN
FLAT = 16
SENT = STATE + 16

EXACT = lax.Precision.HIGHEST
MESH = pl.DeviceIdType.MESH
f32 = jnp.float32
bf16 = jnp.bfloat16


def sigmoid(value):
    return 1.0 / (1.0 + jnp.exp(-value))


def split(value, count):
    pieces = []
    for _ in range(count):
        piece = value.astype(bf16)
        pieces.append(piece)
        value = value - piece.astype(f32)
    return pieces


def remote(src, dst, send, recv, to):
    return pltpu.make_async_remote_copy(
        src_ref=src, dst_ref=dst, send_sem=send, recv_sem=recv, device_id=to, device_id_type=MESH
    )


INPUTS = (
    "entry", "gate", "step", "step_bias", "decay_log", "taps", "tap_bias", "skip", "mixer_gain",
    "residual", "expert_norm", "router", "ids", "w_gate", "w_up", "w_down",
)


def scratch():
    vmem = pltpu.VMEM
    dma = pltpu.SemaphoreType.DMA
    return {
        "padded": vmem((BLOCK + 16, CONV), bf16),
        "gate_v": vmem((BLOCK, D), bf16),
        "step_v": vmem((HEADS, BLOCK), f32),
        "step_bias_v": vmem((1, HEADS), f32),
        "decay_log_v": vmem((1, HEADS), f32),
        "taps_v": vmem((KERNEL, CONV), f32),
        "tap_bias_v": vmem((1, CONV), f32),
        "mixer_gain_v": vmem((1, D), f32),
        "residual_v": vmem((BLOCK, D), bf16),
        "expert_norm_v": vmem((1, D), f32),
        "router_v": vmem((EXPERTS, D), bf16),
        "ids_v": vmem((TOPK, BLOCK), jnp.int32),
        "mixed": vmem((BLOCK, CONV), bf16),
        "cum": vmem((HEADS, BLOCK), f32),
        "delta": vmem((HEADS, BLOCK), f32),
        "cum_cols": vmem((BLOCK, 3 * HEADS), bf16),
        "tail_cols": vmem((BLOCK, 2 * HEADS), bf16),
        "entry_cols": vmem((BLOCK, 2 * HEADS), bf16),
        "last_rows": vmem((16, HEADS), bf16),
        "gram": vmem((BLOCK, BLOCK), f32),
        "piece": vmem((COLUMN, SENT, TILE), bf16),
        "first": vmem((COLUMN, SENT, TILE), bf16),
        "earlier": vmem((COLUMN, STATE, TILE), f32),
        "earlier_log": vmem((COLUMN, 8, TILE), f32),
        "total": vmem((SENT, TILE), bf16),
        "second": vmem((FLAT, SENT, TILE), bf16),
        "third": vmem((COLUMN, STATE, TILE), bf16),
        "state": vmem((COLUMN, STATE, TILE), bf16),
        "before": vmem((STATE, TILE), f32),
        "value": vmem((BLOCK, D), f32),
        "hidden": vmem((BLOCK, D), bf16),
        "rows": vmem((16 * BLOCK, D), bf16),
        "meta": vmem((16, EXPERTS, BLOCK), f32),
        "wg": vmem((D, FF), bf16),
        "wu": vmem((D, FF), bf16),
        "wd": vmem((FF, D), bf16),
        "picked": vmem((4, 2 * PICK, D), bf16),
        "lent": vmem((4, PICK, D), bf16),
        "activated": vmem((2 * PICK, FF), bf16),
        "own_y": vmem((PICK, D), bf16),
        "lent_y": vmem((4, PICK, D), bf16),
        "back_y": vmem((4, PICK, D), bf16),
        "select": vmem((4, 2 * PICK, WIDE), bf16),
        "gate_col": vmem((4, 2 * PICK, BLOCK), f32),
        "part": vmem((16 * BLOCK, D), bf16),
        "land": vmem((15 * BLOCK, D), bf16),
        "done": vmem((BLOCK, D), bf16),
        "load_sem": dma((16,)),
        "halo_send": dma((1,)),
        "halo_recv": dma((1,)),
        "first_send": dma((COLUMN,)),
        "first_recv": dma((COLUMN,)),
        "second_send": dma((FLAT,)),
        "second_recv": dma((FLAT,)),
        "third_send": dma((COLUMN,)),
        "third_recv": dma((COLUMN,)),
        "row_send": dma((30,)),
        "row_recv": dma((30,)),
        "meta_send": dma((15,)),
        "meta_recv": dma((15,)),
        "lent_send": dma((4,)),
        "lent_recv": dma((4,)),
        "back_send": dma((4,)),
        "back_recv": dma((4,)),
        "sum_send": dma((30,)),
        "sum_recv": dma((30,)),
    }


def layer_kernel(*refs):
    names = INPUTS + ("out",) + tuple(scratch())
    r = types.SimpleNamespace(**dict(zip(names, refs)))
    ctx = lax.axis_index("ctx")
    depth = lax.axis_index("exp")
    core = ctx % 2
    column = ctx // 2
    me = core * 4 + depth
    finish = mix_rows(r, ctx, depth, core, column, me)
    spread_rows(r, ctx, depth, core, column)
    finish()


def mix_rows(r, ctx, depth, core, column, me):
    def member(m):
        return (column * 2 + m // 4, m % 4)

    def peer(c):
        return (c * 2 + core, depth)

    last = (me == COLUMN - 1).astype(jnp.int32)
    after = (((column + last) % FLAT) * 2 + ((me + 1) % COLUMN) // 4, (me + 1) % 4)
    initial = (me == 0).astype(jnp.int32)
    ahead = (
        ((column - initial + FLAT) % FLAT) * 2 + ((me + COLUMN - 1) % COLUMN) // 4,
        (me + COLUMN - 1) % 4,
    )

    def load(i, src, dst):
        copy = pltpu.make_async_copy(src, dst, r.load_sem.at[i])
        copy.start()
        return copy

    load_entry = load(0, r.entry, r.padded.at[pl.ds(16, BLOCK)])
    load_steps = [
        load(1, r.step, r.step_v),
        load(2, r.step_bias, r.step_bias_v),
        load(3, r.decay_log, r.decay_log_v),
    ]
    load_taps = [load(4, r.taps, r.taps_v), load(5, r.tap_bias, r.tap_bias_v)]
    load_rest = [
        load(6, r.gate, r.gate_v),
        load(7, r.residual, r.residual_v),
        load(8, r.mixer_gain, r.mixer_gain_v),
        load(9, r.expert_norm, r.expert_norm_v),
        load(10, r.router, r.router_v),
        load(11, r.ids, r.ids_v),
    ]
    for i, (src, dst) in enumerate(((r.w_gate, r.wg), (r.w_up, r.wu), (r.w_down, r.wd))):
        load(12 + i, src.at[0], dst)

    barrier = pltpu.get_barrier_semaphore()

    @pl.loop(1, COLUMN)
    def _(i):
        pl.semaphore_signal(
            barrier, inc=1, device_id=member((me + i) % COLUMN), device_id_type=MESH
        )

    @pl.loop(1, FLAT)
    def _(i):
        pl.semaphore_signal(
            barrier, inc=1, device_id=peer((column + i) % FLAT), device_id_type=MESH
        )

    @pl.when(me == COLUMN - 1)
    def _():
        pl.semaphore_signal(barrier, inc=1, device_id=after, device_id_type=MESH)

    @pl.when(me == 0)
    def _():
        pl.semaphore_signal(barrier, inc=1, device_id=ahead, device_id_type=MESH)

    load_entry.wait()
    pl.semaphore_wait(barrier, COLUMN + FLAT - 2 + last + initial)

    halo = remote(
        r.padded.at[pl.ds(BLOCK, 16)],
        r.padded.at[pl.ds(0, 16)],
        r.halo_send.at[0],
        r.halo_recv.at[0],
        after,
    )
    halo.start()

    row_id = lax.broadcasted_iota(jnp.int32, (BLOCK, BLOCK), 0)
    lane_id = lax.broadcasted_iota(jnp.int32, (BLOCK, BLOCK), 1)
    square_id = [lax.broadcasted_iota(jnp.int32, (HEADS, HEADS), axis) for axis in (0, 1)]

    def upend(row):
        spot = jnp.where(square_id[0] == square_id[1], row, 0.0)
        return jnp.sum(spot, axis=1, keepdims=True)

    for copy in load_steps:
        copy.wait()
    shifted = r.step_v[...] + upend(r.step_bias_v[...])
    width = jnp.maximum(shifted, 0.0) + jnp.log1p(jnp.exp(-jnp.abs(shifted)))
    logs = -width * jnp.exp(upend(r.decay_log_v[...]))
    summed = jnp.dot(
        logs, (row_id <= lane_id).astype(f32), precision=EXACT, preferred_element_type=f32
    )
    r.cum[...] = summed
    r.delta[...] = width

    def upright(a):
        return jnp.concatenate([a, jnp.zeros((BLOCK - HEADS, BLOCK), f32)], axis=0).T[:, :HEADS]

    summed_t = upright(summed)
    width_t = upright(width)
    final = summed_t[BLOCK - 1 :, :]
    r.cum_cols[...] = jnp.concatenate(split(summed_t, 3), axis=1)
    r.tail_cols[...] = jnp.concatenate(split(jnp.exp(final - summed_t) * width_t, 2), axis=1)
    r.entry_cols[...] = jnp.concatenate(split(jnp.exp(summed_t), 2), axis=1)
    terms = split(final, 3)
    r.last_rows[...] = jnp.concatenate(
        terms + [jnp.zeros((13, HEADS), bf16)], axis=0
    )

    def spread(m, copies, per, count):
        head = lax.broadcasted_iota(jnp.int32, (HEADS, count), 0)
        lane = lax.broadcasted_iota(jnp.int32, (HEADS, count), 1)
        one = (head == 4 * m + lane // per).astype(bf16)
        return one if copies == 1 else jnp.concatenate([one] * copies, axis=0)

    for copy in load_taps:
        copy.wait()

    def convolve(full, count, cols):
        acc = jnp.broadcast_to(r.tap_bias_v[:, cols], (count, 128))
        for j in range(KERNEL):
            acc = acc + r.taps_v[j : j + 1, cols] * full[13 + j : 13 + j + count]
        return (acc * sigmoid(acc)).astype(bf16)

    @pl.loop(0, CONV // 128)
    def _(n):
        cols = pl.ds(pl.multiple_of(n * 128, 128), 128)
        r.mixed[16:, cols] = convolve(r.padded[16:, cols].astype(f32), BLOCK - 16, cols)

    halo.wait_recv()
    keep = (ctx + depth > 0).astype(f32)

    @pl.loop(0, CONV // 128)
    def _(n):
        cols = pl.ds(pl.multiple_of(n * 128, 128), 128)
        full = jnp.concatenate(
            [r.padded[0:16, cols].astype(f32) * keep, r.padded[16:32, cols].astype(f32)], axis=0
        )
        r.mixed[0:16, cols] = convolve(full, 16, cols)

    in_map = r.mixed[:, D : D + STATE]
    out_map = r.mixed[:, D + STATE : D + 2 * STATE]
    in_twice = jnp.concatenate([in_map, in_map], axis=0)

    def first_copy(m, slot):
        return remote(
            r.piece.at[m], r.first.at[slot], r.first_send.at[m], r.first_recv.at[slot], member(m)
        )

    @pl.loop(0, COLUMN)
    def _(i):
        m = (me + 1 + i) % COLUMN
        cols = pl.ds(pl.multiple_of(m * TILE, TILE), TILE)
        weight = jnp.dot(r.tail_cols[...], spread(m, 2, HEAD_DIM, TILE), preferred_element_type=f32)
        weighted = r.mixed[:, cols].astype(f32) * weight
        r.piece[m, 0:STATE, :] = lax.dot_general(
            in_twice,
            jnp.concatenate(split(weighted, 2), axis=0),
            (((0,), (0,)), ((), ())),
            preferred_element_type=f32,
        ).astype(bf16)
        r.piece[m, STATE:, :] = jnp.dot(
            r.last_rows[...], spread(m, 1, HEAD_DIM, TILE), preferred_element_type=f32
        ).astype(bf16)

        @pl.when(i < COLUMN - 1)
        def _():
            first_copy(m, me).start()

    r.first[me] = r.piece[me]

    cross = lax.dot_general(
        out_map, in_map, (((1,), (1,)), ((), ())), preferred_element_type=f32
    )
    r.gram[...] = jnp.where(row_id >= lane_id, cross, 0.0)

    def inside(m):
        cols = pl.ds(pl.multiple_of(m * TILE, TILE), TILE)
        upto = jnp.dot(r.cum_cols[...], spread(m, 3, BLOCK, 4 * BLOCK), preferred_element_type=f32)
        feature = r.mixed[:, cols]
        lane = lax.broadcasted_iota(jnp.int32, (BLOCK, TILE), 1) // HEAD_DIM
        highs, lows, blocks = [], [], []
        for j in range(4):
            head = pl.ds(4 * m + j, 1)
            gap = upto[:, BLOCK * j : BLOCK * (j + 1)] - r.cum[head, :]
            mix = jnp.exp(jnp.minimum(gap, 0.0)) * r.gram[...] * r.delta[head, :]
            mix = mix + jnp.where(row_id == lane_id, r.skip[4 * m + j], 0.0)
            high, low = split(mix, 2)
            highs.append(high)
            lows.append(low)
            blocks.append(jnp.where(lane == j, feature, jnp.zeros_like(feature)))
        diagonal = jnp.concatenate(blocks, axis=0)
        r.value[:, cols] = jnp.dot(
            jnp.concatenate(highs, axis=1), diagonal, preferred_element_type=f32
        ) + jnp.dot(jnp.concatenate(lows, axis=1), diagonal, preferred_element_type=f32)

    @pl.loop(0, COLUMN)
    def _(m):
        inside(m)

    @pl.loop(0, COLUMN)
    def _(m):
        @pl.when(m != me)
        def _():
            first_copy(m, m).wait_recv()

    def log_of(block):
        terms = block.astype(f32)
        return terms[0:1] + terms[1:2] + terms[2:3]

    run = jnp.zeros((STATE, TILE), f32)
    run_log = jnp.zeros((1, TILE), f32)
    for m in range(COLUMN):
        r.earlier[m] = run
        r.earlier_log[m] = jnp.broadcast_to(run_log, (8, TILE))
        log = log_of(r.first[m, STATE:, :])
        run = run * jnp.exp(log) + r.first[m, 0:STATE, :].astype(f32)
        run_log = run_log + log
    r.total[0:STATE, :] = run.astype(bf16)
    r.total[STATE:, :] = jnp.concatenate(
        split(run_log, 3) + [jnp.zeros((13, TILE), bf16)], axis=0
    )

    def second_copy(o):
        return remote(
            r.total,
            r.second.at[o],
            r.second_send.at[o],
            r.second_recv.at[o],
            peer((column + o) % FLAT),
        )

    @pl.loop(1, FLAT)
    def _(o):
        @pl.when(column + o < FLAT)
        def _():
            second_copy(o).start()

    for copy in load_rest:
        copy.wait()
    r.before[...] = jnp.zeros((STATE, TILE), f32)

    @pl.loop(1, FLAT)
    def _(i):
        o = FLAT - i

        @pl.when(o <= column)
        def _():
            second_copy(o).wait_recv()
            r.before[...] = (
                r.before[...] * jnp.exp(log_of(r.second[o, STATE:, :]))
                + r.second[o, 0:STATE, :].astype(f32)
            )

    def third_copy(m, slot):
        return remote(
            r.third.at[m], r.state.at[slot], r.third_send.at[m], r.third_recv.at[slot], member(m)
        )

    @pl.loop(0, COLUMN)
    def _(i):
        m = (me + 1 + i) % COLUMN
        r.third[m] = (r.before[...] * jnp.exp(r.earlier_log[m, 0:1, :]) + r.earlier[m]).astype(bf16)

        @pl.when(i < COLUMN - 1)
        def _():
            third_copy(m, me).start()

    r.state[me] = r.third[me]

    @pl.loop(0, COLUMN)
    def _(m):
        @pl.when(m != me)
        def _():
            third_copy(m, m).wait_recv()

    def fold(a):
        return a[:, :128] + a[:, 128:]

    def carry(m, square):
        cols = pl.ds(pl.multiple_of(m * TILE, TILE), TILE)
        carried = jnp.dot(out_map, r.state[m], preferred_element_type=f32)
        weight = jnp.dot(r.entry_cols[...], spread(m, 2, HEAD_DIM, TILE), preferred_element_type=f32)
        branch = r.gate_v[:, cols].astype(f32)
        v = (r.value[:, cols] + carried * weight) * (branch * sigmoid(branch))
        r.value[:, cols] = v
        return square + fold(v * v)

    zero = jnp.zeros((BLOCK, 128), f32)
    square = lax.fori_loop(0, COLUMN, carry, zero)
    scale = lax.rsqrt(jnp.sum(square, axis=1, keepdims=True) * (1.0 / D) + 1e-05)

    def join(m, square):
        cols = pl.ds(pl.multiple_of(m * TILE, TILE), TILE)
        out = r.value[:, cols] * scale * r.mixer_gain_v[:, cols]
        kept = (r.residual_v[:, cols].astype(f32) + out).astype(bf16)
        r.hidden[:, cols] = kept
        wide = kept.astype(f32)
        return square + fold(wide * wide)

    square = lax.fori_loop(0, COLUMN, join, zero)
    again = lax.rsqrt(jnp.sum(square, axis=1, keepdims=True) * (1.0 / D) + 1e-05)

    @pl.loop(0, COLUMN)
    def _(m):
        cols = pl.ds(pl.multiple_of(m * TILE, TILE), TILE)
        r.rows[0:BLOCK, cols] = (
            r.hidden[:, cols].astype(f32) * again * r.expert_norm_v[:, cols]
        ).astype(bf16)

    logits = lax.dot_general(
        r.router_v[...], r.rows[0:BLOCK, :], (((1,), (1,)), ((), ())), preferred_element_type=f32
    )
    expert = lax.broadcasted_iota(jnp.int32, (EXPERTS, BLOCK), 0)
    chosen = expert < 0
    for k in range(TOPK):
        chosen = chosen | (expert == r.ids_v[k : k + 1, :])
    score = jnp.where(chosen, sigmoid(logits), 0.0)
    r.meta[0] = score / jnp.sum(score, axis=0, keepdims=True)

    def finish():
        halo.wait_send()

        @pl.loop(0, COLUMN)
        def _(m):
            @pl.when(m != me)
            def _():
                first_copy(m, me).wait_send()
                third_copy(m, me).wait_send()

        @pl.loop(1, FLAT)
        def _(o):
            @pl.when(column + o < FLAT)
            def _():
                second_copy(o).wait_send()

    return finish


def spread_rows(r, ctx, depth, core, column):
    x = column % 4
    y = column // 4
    sibling = ctx + 1 - 2 * core

    def device(first, second):
        to_y = (y + core * first + (1 - core) * second + 4) % 4
        to_x = (x + core * second + (1 - core) * first + 4) % 4
        return ((to_y * 4 + to_x) * 2 + core, depth)

    forth = (device(1, 0), device(0, 1))
    back = (device(-1, 0), device(0, -1))
    across = (sibling, depth)

    def ring(stage):
        return (0, 4, 0) if stage == 0 else (4 * (stage - 1), 1, 1)

    def row_copy(stage, kind):
        base, stride, axis = ring(stage)
        sem = 6 * stage + kind
        to = (forth, back)[kind % 2][axis]
        source, target, low = (
            (0, 1, 0), (0, 3, HALF), (0, 1, HALF), (0, 3, 0), (1, 2, 0), (3, 2, HALF)
        )[kind]
        return remote(
            r.rows.at[pl.ds((base + stride * source) * BLOCK + low, HALF)],
            r.rows.at[pl.ds((base + stride * target) * BLOCK + low, HALF)],
            r.row_send.at[sem],
            r.row_recv.at[sem],
            to,
        )

    def meta_copy(stage, kind):
        base, stride, axis = ring(stage)
        sem = 3 * stage + kind
        source, target, to = ((0, 1, forth), (0, 3, back), (1, 2, forth))[kind]
        return remote(
            r.meta.at[base + stride * source],
            r.meta.at[base + stride * target],
            r.meta_send.at[sem],
            r.meta_recv.at[sem],
            to[axis],
        )

    def sum_copy(stage, kind):
        base, stride, axis = ring(stage)
        sem = 6 * stage + kind
        to = (back, forth)[kind % 2][axis]
        source, low, place = (
            (2, 0, 0),
            (2, HALF, HALF),
            (1, HALF, BLOCK + HALF),
            (3, 0, 2 * BLOCK),
            (1, 0, BLOCK),
            (3, HALF, 2 * BLOCK + HALF),
        )[kind]
        return remote(
            r.part.at[pl.ds((base + stride * source) * BLOCK + low, HALF)],
            r.land.at[pl.ds(stage * 3 * BLOCK + place, HALF)],
            r.sum_send.at[sem],
            r.sum_recv.at[sem],
            to,
        )

    def lent_copy(k):
        return remote(
            r.lent.at[k],
            r.picked.at[k, pl.ds(PICK, PICK)],
            r.lent_send.at[k],
            r.lent_recv.at[k],
            across,
        )

    def back_copy(k):
        return remote(
            r.lent_y.at[k], r.back_y.at[k], r.back_send.at[k], r.back_recv.at[k], across
        )

    def send_rows(stage, *kinds):
        for kind in kinds:
            row_copy(stage, kind).start()

    def send_meta(stage):
        meta_copy(stage, 0).start()
        meta_copy(stage, 1).start()

    def pass_rows(stage, kind):
        row_copy(stage, kind).wait_recv()
        row_copy(stage, kind + 4).start()

    def pass_both(stage):
        meta_copy(stage, 0).wait_recv()
        meta_copy(stage, 2).start()
        pass_rows(stage, 0)
        pass_rows(stage, 1)

    def arrive(stage):
        for kind in (1, 2):
            meta_copy(stage, kind).wait_recv()
        for kind in (2, 3, 4, 5):
            row_copy(stage, kind).wait_recv()

    before = (
        lax.broadcasted_iota(jnp.int32, (BLOCK, BLOCK), 0)
        < lax.broadcasted_iota(jnp.int32, (BLOCK, BLOCK), 1)
    ).astype(bf16)
    slot_row = lax.broadcasted_iota(jnp.int32, (PICK, WIDE), 0).astype(f32)

    def choose(k):
        gate = jnp.concatenate(
            [
                r.meta[4 * k + j, pl.ds(expert, 1), :]
                for expert in (ctx, sibling)
                for j in range(4)
            ],
            axis=0,
        )
        live = gate > 0.0
        rank = jnp.dot(live.astype(bf16), before, preferred_element_type=f32)
        shift = (lax.broadcasted_iota(jnp.int32, (8, BLOCK), 0) % 4).astype(f32) * CAP
        slot = jnp.where(live, rank + shift, -1.0)
        for half in range(2):
            lanes = jnp.concatenate([slot[4 * half + j : 4 * half + j + 1] for j in range(4)], axis=1)
            value = jnp.concatenate([gate[4 * half + j : 4 * half + j + 1] for j in range(4)], axis=1)
            hit = slot_row == lanes
            span = pl.ds(half * PICK, PICK)
            r.select[k, span, :] = jnp.where(hit, 1.0, 0.0).astype(bf16)
            total = jnp.sum(jnp.where(hit, value, 0.0), axis=1, keepdims=True)
            r.gate_col[k, span, :] = jnp.broadcast_to(total, (PICK, BLOCK))

        @pl.loop(0, 8)
        def _(n):
            cols = pl.ds(pl.multiple_of(n * 256, 256), 256)
            got = jnp.dot(
                r.select[k], r.rows[pl.ds(k * WIDE, WIDE), cols], preferred_element_type=f32
            ).astype(bf16)
            r.picked[k, pl.ds(0, PICK), cols] = got[:PICK]
            r.lent[k, :, cols] = got[PICK:]

        lent_copy(k).start()

    def feed(k):
        lent_copy(k).wait_recv()

        @pl.loop(0, 3)
        def _(f):
            cols = pl.ds(pl.multiple_of(f * 256, 256), 256)
            gate = jnp.dot(r.picked[k], r.wg[:, cols], preferred_element_type=f32)
            up = jnp.dot(r.picked[k], r.wu[:, cols], preferred_element_type=f32)
            r.activated[:, cols] = (gate * sigmoid(gate) * up).astype(bf16)

    def produce(k):
        @pl.loop(0, 8)
        def _(n):
            cols = pl.ds(pl.multiple_of(n * 256, 256), 256)
            made = jnp.dot(r.activated[...], r.wd[:, cols], preferred_element_type=f32)
            scale = r.gate_col[k, pl.ds(0, PICK), :]
            r.own_y[:, cols] = (
                made[:PICK] * jnp.concatenate([scale, scale], axis=1)
            ).astype(bf16)
            r.lent_y[k, :, cols] = made[PICK:].astype(bf16)

        back_copy(k).start()

    def combine(k):
        back_copy(k).wait_recv()

        @pl.loop(0, 8)
        def _(n):
            cols = pl.ds(pl.multiple_of(n * 256, 256), 256)
            scale = r.gate_col[k, pl.ds(PICK, PICK), :]
            other = (
                r.back_y[k, :, cols].astype(f32) * jnp.concatenate([scale, scale], axis=1)
            ).astype(bf16)
            both = jnp.concatenate([r.own_y[:, cols], other], axis=0)
            r.part[pl.ds(k * WIDE, WIDE), cols] = lax.dot_general(
                r.select[k], both, (((0,), (0,)), ((), ())), preferred_element_type=f32
            ).astype(bf16)

    def add_into(block, low, count, places):
        @pl.loop(0, count // 16)
        def _(i):
            span = pl.ds(pl.multiple_of(block * BLOCK + low + i * 16, 16), 16)
            total = r.part[span, :].astype(f32)
            for place in places:
                total += r.land[pl.ds(pl.multiple_of(place + i * 16, 16), 16), :].astype(f32)
            r.part[span, :] = total.astype(bf16)

    def sum_first(stage):
        for kind in range(4):
            sum_copy(stage, kind).start()

    def sum_second(stage):
        base, stride, _ = ring(stage)
        place = stage * 3 * BLOCK
        sum_copy(stage, 0).wait_recv()
        add_into(base + stride, 0, HALF, (place,))
        sum_copy(stage, 4).start()
        sum_copy(stage, 1).wait_recv()
        add_into(base + 3 * stride, HALF, HALF, (place + HALF,))
        sum_copy(stage, 5).start()

    def sum_last(stage):
        base, _, _ = ring(stage)
        place = stage * 3 * BLOCK
        for kind in (2, 3, 4, 5):
            sum_copy(stage, kind).wait_recv()
        if stage > 0:
            add_into(base, 0, BLOCK, (place + BLOCK, place + 2 * BLOCK))

    send_meta(0)
    send_rows(0, 0, 1, 2, 3)
    send_meta(1)
    send_rows(1, 0, 1)
    meta_copy(0, 0).wait_recv()
    meta_copy(0, 2).start()
    send_meta(2)
    pass_rows(0, 0)
    send_rows(2, 0, 3)
    meta_copy(0, 1).wait_recv()
    send_meta(4)
    pass_rows(0, 1)
    send_rows(4, 1, 2)
    send_rows(1, 2, 3)
    row_copy(0, 2).wait_recv()
    send_rows(2, 1, 2)
    row_copy(0, 3).wait_recv()
    send_rows(4, 0, 3)
    pass_both(1)
    meta_copy(0, 2).wait_recv()
    send_meta(3)
    row_copy(0, 4).wait_recv()
    send_rows(3, 0, 3)
    row_copy(0, 5).wait_recv()
    send_rows(3, 1, 2)
    pass_both(2)
    pass_both(4)
    arrive(1)
    choose(0)
    for i, (src, dst) in enumerate(((r.w_gate, r.wg), (r.w_up, r.wu), (r.w_down, r.wd))):
        pltpu.make_async_copy(src.at[0], dst, r.load_sem.at[12 + i]).wait()
    feed(0)
    pass_both(3)
    produce(0)
    arrive(2)
    choose(1)
    combine(0)
    feed(1)
    produce(1)
    arrive(4)
    choose(3)
    combine(1)
    sum_first(2)
    feed(3)
    produce(3)
    arrive(3)
    choose(2)
    combine(3)
    sum_first(4)
    sum_second(2)
    feed(2)
    produce(2)
    sum_second(4)
    combine(2)
    sum_first(3)
    sum_first(1)
    sum_last(2)
    sum_last(4)
    sum_second(3)
    sum_second(1)
    sum_last(3)
    sum_first(0)
    sum_last(1)
    sum_second(0)
    sum_last(0)

    @pl.loop(0, BLOCK // 16)
    def _(i):
        span = pl.ds(pl.multiple_of(i * 16, 16), 16)
        total = r.part[span, :].astype(f32)
        for place in (BLOCK, 2 * BLOCK):
            total += r.land[pl.ds(pl.multiple_of(place + i * 16, 16), 16), :].astype(f32)
        r.done[span, :] = (r.hidden[span, :].astype(f32) + total).astype(bf16)

    store = pltpu.make_async_copy(r.done, r.out, r.load_sem.at[15])
    store.start()
    for stage in range(5):
        for kind in range(6):
            row_copy(stage, kind).wait_send()
            sum_copy(stage, kind).wait_send()
        for kind in range(3):
            meta_copy(stage, kind).wait_send()
    for k in range(4):
        lent_copy(k).wait_send()
        back_copy(k).wait_send()
    store.wait()


def layer(
    filter_entry_array,
    gate_input,
    step_unshifted,
    step_bias,
    decay_log,
    conv_weight,
    conv_bias,
    skip_gain,
    mixer_gain,
    residual,
    expert_norm,
    router_weight,
    expert_ids,
    w_gate,
    w_up,
    w_down,
):
    hbm = pl.BlockSpec(memory_space=pl.ANY)
    specs = [hbm] * len(INPUTS)
    specs[INPUTS.index("skip")] = pl.BlockSpec(memory_space=pltpu.SMEM)
    return pl.pallas_call(
        layer_kernel,
        out_shape=jax.ShapeDtypeStruct((BLOCK, D), bf16),
        in_specs=specs,
        out_specs=hbm,
        scratch_shapes=list(scratch().values()),
        compiler_params=pltpu.CompilerParams(
            collective_id=0, has_side_effects=True, vmem_limit_bytes=62 * 1024 * 1024
        ),
    )(
        filter_entry_array,
        gate_input,
        step_unshifted,
        step_bias[None, :],
        decay_log[None, :],
        conv_weight,
        conv_bias[None, :],
        skip_gain,
        mixer_gain[None, :],
        residual,
        expert_norm[None, :],
        router_weight.T,
        expert_ids.T,
        w_gate,
        w_up,
        w_down,
    )


def solution(mesh):
    rows = P(("ctx", "exp"), None)
    shared = P()
    owner = P("ctx", None, None)
    return jax.shard_map(
        layer,
        mesh=mesh,
        in_specs=(
            rows,
            rows,
            P(None, ("ctx", "exp")),
            shared,
            shared,
            shared,
            shared,
            shared,
            shared,
            rows,
            shared,
            shared,
            rows,
            owner,
            owner,
            owner,
        ),
        out_specs=rows,
        check_vma=False,
    )
```

time: 874 us -> 152 us (0.17); the launches traced: 864 us -> 152 us
  blocking collectives: 476 us -> 0 us
  waiting for transfers between devices: 260 us -> 0 us
  Pallas kernels: 0 us -> 149 us
  local copies, waits for them, and re-layouts: 45.1 us -> 3.19 us
  matrix products: 32.8 us -> 0 us
  other arithmetic: 27.3 us -> 0 us
  between operations: 13.7 us -> 0.01 us
  starting transfers between devices: 9.3 us -> 0 us
    all_to_all x1 -> x0, blocking collectives: 409 us -> none  [body(): lax.all_to_all(outgoing, 'ctx', split_axis=0, concat_axis=0, tiled=True)]
    all_gather x1 -> x0, waiting for transfers between devices: 203 us -> none  [prefix(): gathered = jax.tree.map(lambda a: lax.all_gather(a, axis), part)]
    pallas_call x0 -> x1, Pallas kernels: none -> 149 us  [layer(): pl.pallas_call(layer_kernel, out_shape=jax.ShapeDtypeStruct((BLOCK, D), b...]
    unnamed x1 -> x0, blocking collectives: 67.5 us -> none
    all_to_all x1 -> x0, waiting for transfers between devices: 56.6 us -> none  [body(): lax.all_to_all(produced.reshape(sources * local_experts, slot_count, D),...]
    dot_general x7 -> x0, matrix products: 32.8 us -> none  [the longest x1 14.7 us: body(): jnp.einsum('sekf,efd->sekd', activated, w_down, preferred_element_type=jn...]
    gather x6 -> x0, local copies, waits for them, and re-layouts: 19.3 us -> none  [the longest x1 12 us: body(): returned.reshape(experts_all * CAP, D)[destination].astype(jnp.float32)]
    reduce_sum x5 -> x0, other arithmetic: 10.6 us -> none  [the longest x1 6.57 us: body(): expert_sum = jnp.sum(gates[:, :, None] * picked, axis=1)]
  transfers between devices with their start and end apart: 3 -> 0, of which waited for: 2 -> 0; matrix products, arithmetic and copies ran while one was open for 3% -> 0% of each run, Pallas kernels for 0% -> 0%
where the time goes in v4:
time: 152 us
  Pallas kernels  149 us (98%)
  local copies, waits for them, and re-layouts  3.19 us (2%)
    pallas_call x1, Pallas kernels, layer(): pl.pallas_call(layer_kernel, out_shape=jax.ShapeDtypeStruct((BLOCK, D), b...  149 us

profile of v4, /device:TPU:0, one launch (start us, length us, event | category | flops | bytes accessed | tf_op | source)
XLA Modules:
  0.0 152.0 jit_solution(13730420123963471216)
XLA Ops:
  0.0 1.3 broadcast_in_dim.17.refs_6_
  1.3 148.8 %shard_map.154 = bf16[128,2048]{1,0:T(8,128)(2,1)} custom-call(bf16[128,2176]{1,0:T(8,128)(2,1)} %refs_0_.1, bf16[128,2048]{1,0:T(8,128)(2,1)} %refs_1_.1, f32[32,128]{1,0:T(8,128)} %refs_2_.1, f32[1,32]{1,0:T(1,128)} %bitcast.10, f32[1,32]{1,0:T(1,128)} %bitcast.11, f32[4,2176]{1,0:T(4,128)} %refs_5_.1, f32[1,2176]{1,0:T(1,128)} %broadcast_in_dim.17.refs_6_, ...), custom_call_target="tpu_custom_call" | custom-call | tf_op jit(solution)/shard_map/pallas_call | solution.py:800
  150.2 1.9 %copy.18 = bf16[128,2048]{1,0:T(8,128)(2,1)} copy(bf16[128,2048]{1,0:T(8,128)(2,1)} %shard_map.154) | data formatting | bytes 1048576

commit v5 on v4

--- a/solution.py
+++ b/solution.py
@@ -67,7 +67,7 @@
         "step_bias_v": vmem((1, HEADS), f32),
         "decay_log_v": vmem((1, HEADS), f32),
         "taps_v": vmem((KERNEL, CONV), f32),
-        "tap_bias_v": vmem((1, CONV), f32),
+        "tap_bias_v": vmem((CONV,), f32),
         "mixer_gain_v": vmem((1, D), f32),
         "residual_v": vmem((BLOCK, D), bf16),
         "expert_norm_v": vmem((1, D), f32),
@@ -91,6 +91,7 @@
         "state": vmem((COLUMN, STATE, TILE), bf16),
         "before": vmem((STATE, TILE), f32),
         "value": vmem((BLOCK, D), f32),
+        "branch": vmem((BLOCK, D), f32),
         "hidden": vmem((BLOCK, D), bf16),
         "rows": vmem((16 * BLOCK, D), bf16),
         "meta": vmem((16, EXPERTS, BLOCK), f32),
@@ -138,8 +139,8 @@
     core = ctx % 2
     column = ctx // 2
     me = core * 4 + depth
-    finish = mix_rows(r, ctx, depth, core, column, me)
-    spread_rows(r, ctx, depth, core, column)
+    score_rows, finish = mix_rows(r, ctx, depth, core, column, me)
+    spread_rows(r, ctx, depth, core, column, score_rows)
     finish()
 
 
@@ -203,18 +204,6 @@
     def _():
         pl.semaphore_signal(barrier, inc=1, device_id=ahead, device_id_type=MESH)
 
-    load_entry.wait()
-    pl.semaphore_wait(barrier, COLUMN + FLAT - 2 + last + initial)
-
-    halo = remote(
-        r.padded.at[pl.ds(BLOCK, 16)],
-        r.padded.at[pl.ds(0, 16)],
-        r.halo_send.at[0],
-        r.halo_recv.at[0],
-        after,
-    )
-    halo.start()
-
     row_id = lax.broadcasted_iota(jnp.int32, (BLOCK, BLOCK), 0)
     lane_id = lax.broadcasted_iota(jnp.int32, (BLOCK, BLOCK), 1)
     square_id = [lax.broadcasted_iota(jnp.int32, (HEADS, HEADS), axis) for axis in (0, 1)]
@@ -256,9 +245,10 @@
 
     for copy in load_taps:
         copy.wait()
+    load_entry.wait()
 
     def convolve(full, count, cols):
-        acc = jnp.broadcast_to(r.tap_bias_v[:, cols], (count, 128))
+        acc = jnp.broadcast_to(r.tap_bias_v[cols][None, :], (count, 128))
         for j in range(KERNEL):
             acc = acc + r.taps_v[j : j + 1, cols] * full[13 + j : 13 + j + count]
         return (acc * sigmoid(acc)).astype(bf16)
@@ -267,6 +257,43 @@
     def _(n):
         cols = pl.ds(pl.multiple_of(n * 128, 128), 128)
         r.mixed[16:, cols] = convolve(r.padded[16:, cols].astype(f32), BLOCK - 16, cols)
+
+    def weighted(m, low, count):
+        cols = pl.ds(pl.multiple_of(m * TILE, TILE), TILE)
+        span = pl.ds(low, count)
+        weight = jnp.dot(
+            r.tail_cols[span, :], spread(m, 2, HEAD_DIM, TILE), preferred_element_type=f32
+        )
+        source = r.mixed[span, D : D + STATE]
+        return lax.dot_general(
+            jnp.concatenate([source, source], axis=0),
+            jnp.concatenate(split(r.mixed[span, cols].astype(f32) * weight, 2), axis=0),
+            (((0,), (0,)), ((), ())),
+            preferred_element_type=f32,
+        )
+
+    @pl.loop(0, COLUMN)
+    def _(m):
+        r.earlier[m] = weighted(m, 16, BLOCK - 16)
+
+    pl.semaphore_wait(barrier, COLUMN + FLAT - 2 + last + initial)
+    halo = remote(
+        r.padded.at[pl.ds(BLOCK, 16)],
+        r.padded.at[pl.ds(0, 16)],
+        r.halo_send.at[0],
+        r.halo_recv.at[0],
+        after,
+    )
+    halo.start()
+
+    for copy in load_rest:
+        copy.wait()
+
+    @pl.loop(0, COLUMN)
+    def _(m):
+        cols = pl.ds(pl.multiple_of(m * TILE, TILE), TILE)
+        branch = r.gate_v[:, cols].astype(f32)
+        r.branch[:, cols] = branch * sigmoid(branch)
 
     halo.wait_recv()
     keep = (ctx + depth > 0).astype(f32)
@@ -281,25 +308,20 @@
 
     in_map = r.mixed[:, D : D + STATE]
     out_map = r.mixed[:, D + STATE : D + 2 * STATE]
-    in_twice = jnp.concatenate([in_map, in_map], axis=0)
 
     def first_copy(m, slot):
         return remote(
             r.piece.at[m], r.first.at[slot], r.first_send.at[m], r.first_recv.at[slot], member(m)
         )
 
+    def around(i):
+        q = i // 2
+        return ((core + i) % 2) * 4 + (depth + q + q // 2 - 2 * (q // 3)) % 4
+
     @pl.loop(0, COLUMN)
     def _(i):
-        m = (me + 1 + i) % COLUMN
-        cols = pl.ds(pl.multiple_of(m * TILE, TILE), TILE)
-        weight = jnp.dot(r.tail_cols[...], spread(m, 2, HEAD_DIM, TILE), preferred_element_type=f32)
-        weighted = r.mixed[:, cols].astype(f32) * weight
-        r.piece[m, 0:STATE, :] = lax.dot_general(
-            in_twice,
-            jnp.concatenate(split(weighted, 2), axis=0),
-            (((0,), (0,)), ((), ())),
-            preferred_element_type=f32,
-        ).astype(bf16)
+        m = around(COLUMN - 1 - i)
+        r.piece[m, 0:STATE, :] = (r.earlier[m] + weighted(m, 0, 16)).astype(bf16)
         r.piece[m, STATE:, :] = jnp.dot(
             r.last_rows[...], spread(m, 1, HEAD_DIM, TILE), preferred_element_type=f32
         ).astype(bf16)
@@ -372,13 +394,13 @@
         )
 
     @pl.loop(1, FLAT)
-    def _(o):
+    def _(i):
+        o = FLAT - i
+
         @pl.when(column + o < FLAT)
         def _():
             second_copy(o).start()
 
-    for copy in load_rest:
-        copy.wait()
     r.before[...] = jnp.zeros((STATE, TILE), f32)
 
     @pl.loop(1, FLAT)
@@ -400,7 +422,7 @@
 
     @pl.loop(0, COLUMN)
     def _(i):
-        m = (me + 1 + i) % COLUMN
+        m = around(COLUMN - 1 - i)
         r.third[m] = (r.before[...] * jnp.exp(r.earlier_log[m, 0:1, :]) + r.earlier[m]).astype(bf16)
 
         @pl.when(i < COLUMN - 1)
@@ -409,21 +431,20 @@
 
     r.state[me] = r.third[me]
 
-    @pl.loop(0, COLUMN)
-    def _(m):
-        @pl.when(m != me)
+    def fold(a):
+        return a[:, :128] + a[:, 128:]
+
+    def carry(i, square):
+        m = around(i)
+
+        @pl.when(i > 0)
         def _():
             third_copy(m, m).wait_recv()
 
-    def fold(a):
-        return a[:, :128] + a[:, 128:]
-
-    def carry(m, square):
         cols = pl.ds(pl.multiple_of(m * TILE, TILE), TILE)
         carried = jnp.dot(out_map, r.state[m], preferred_element_type=f32)
         weight = jnp.dot(r.entry_cols[...], spread(m, 2, HEAD_DIM, TILE), preferred_element_type=f32)
-        branch = r.gate_v[:, cols].astype(f32)
-        v = (r.value[:, cols] + carried * weight) * (branch * sigmoid(branch))
+        v = (r.value[:, cols] + carried * weight) * r.branch[:, cols]
         r.value[:, cols] = v
         return square + fold(v * v)
 
@@ -449,15 +470,16 @@
             r.hidden[:, cols].astype(f32) * again * r.expert_norm_v[:, cols]
         ).astype(bf16)
 
-    logits = lax.dot_general(
-        r.router_v[...], r.rows[0:BLOCK, :], (((1,), (1,)), ((), ())), preferred_element_type=f32
-    )
-    expert = lax.broadcasted_iota(jnp.int32, (EXPERTS, BLOCK), 0)
-    chosen = expert < 0
-    for k in range(TOPK):
-        chosen = chosen | (expert == r.ids_v[k : k + 1, :])
-    score = jnp.where(chosen, sigmoid(logits), 0.0)
-    r.meta[0] = score / jnp.sum(score, axis=0, keepdims=True)
+    def score_rows():
+        logits = lax.dot_general(
+            r.router_v[...], r.rows[0:BLOCK, :], (((1,), (1,)), ((), ())), preferred_element_type=f32
+        )
+        expert = lax.broadcasted_iota(jnp.int32, (EXPERTS, BLOCK), 0)
+        chosen = expert < 0
+        for k in range(TOPK):
+            chosen = chosen | (expert == r.ids_v[k : k + 1, :])
+        score = jnp.where(chosen, sigmoid(logits), 0.0)
+        r.meta[0] = score / jnp.sum(score, axis=0, keepdims=True)
 
     def finish():
         halo.wait_send()
@@ -475,10 +497,10 @@
             def _():
                 second_copy(o).wait_send()
 
-    return finish
-
-
-def spread_rows(r, ctx, depth, core, column):
+    return score_rows, finish
+
+
+def spread_rows(r, ctx, depth, core, column, score_rows):
     x = column % 4
     y = column // 4
     sibling = ctx + 1 - 2 * core
@@ -688,10 +710,11 @@
         if stage > 0:
             add_into(base, 0, BLOCK, (place + BLOCK, place + 2 * BLOCK))
 
+    send_rows(0, 0, 1, 2, 3)
+    send_rows(1, 0, 1, 2, 3)
+    score_rows()
     send_meta(0)
-    send_rows(0, 0, 1, 2, 3)
     send_meta(1)
-    send_rows(1, 0, 1)
     meta_copy(0, 0).wait_recv()
     meta_copy(0, 2).start()
     send_meta(2)
@@ -700,31 +723,30 @@
     meta_copy(0, 1).wait_recv()
     send_meta(4)
     pass_rows(0, 1)
-    send_rows(4, 1, 2)
-    send_rows(1, 2, 3)
     row_copy(0, 2).wait_recv()
     send_rows(2, 1, 2)
+    pass_both(1)
     row_copy(0, 3).wait_recv()
-    send_rows(4, 0, 3)
-    pass_both(1)
+    send_rows(4, 1, 2, 0, 3)
+    pass_both(2)
     meta_copy(0, 2).wait_recv()
     send_meta(3)
     row_copy(0, 4).wait_recv()
     send_rows(3, 0, 3)
     row_copy(0, 5).wait_recv()
     send_rows(3, 1, 2)
-    pass_both(2)
-    pass_both(4)
     arrive(1)
     choose(0)
     for i, (src, dst) in enumerate(((r.w_gate, r.wg), (r.w_up, r.wu), (r.w_down, r.wd))):
         pltpu.make_async_copy(src.at[0], dst, r.load_sem.at[12 + i]).wait()
+    pass_both(4)
     feed(0)
-    pass_both(3)
     produce(0)
     arrive(2)
     choose(1)
     combine(0)
+    pass_both(3)
+    sum_first(1)
     feed(1)
     produce(1)
     arrive(4)
@@ -743,7 +765,6 @@
     sum_second(4)
     combine(2)
     sum_first(3)
-    sum_first(1)
     sum_last(2)
     sum_last(4)
     sum_second(3)
@@ -813,7 +834,7 @@
         step_bias[None, :],
         decay_log[None, :],
         conv_weight,
-        conv_bias[None, :],
+        conv_bias,
         skip_gain,
         mixer_gain[None, :],
         residual,

time: 152 us -> 140 us (0.921)
  Pallas kernels: 149 us -> 138 us
    pallas_call x1, Pallas kernels: 149 us -> 138 us  [layer(): pl.pallas_call(layer_kernel, out_shape=jax.ShapeDtypeStruct((BLOCK, D), b...]
where the time goes in v5:
time: 140 us
  Pallas kernels  138 us (99%)
  local copies, waits for them, and re-layouts  1.88 us (1%)
    pallas_call x1, Pallas kernels, layer(): pl.pallas_call(layer_kernel, out_shape=jax.ShapeDtypeStruct((BLOCK, D), b...  138 us

profile of v5, /device:TPU:0, one launch (start us, length us, event | category | flops | bytes accessed | tf_op | source)
XLA Modules:
  0.0 140.0 jit_solution(7721132763619196099)
XLA Ops:
  0.0 138.2 %shard_map.154 = bf16[128,2048]{1,0:T(8,128)(2,1)} custom-call(bf16[128,2176]{1,0:T(8,128)(2,1)} %refs_0_.1, bf16[128,2048]{1,0:T(8,128)(2,1)} %refs_1_.1, f32[32,128]{1,0:T(8,128)} %refs_2_.1, f32[1,32]{1,0:T(1,128)} %bitcast.10, f32[1,32]{1,0:T(1,128)} %bitcast.11, f32[4,2176]{1,0:T(4,128)} %refs_5_.1, f32[2176]{0:T(1024)} %refs_6_.1, f32[32]{0:T(128)} %refs_7_.1, ...), custom_call_target="tpu_custom_call" | custom-call | tf_op jit(solution)/shard_map/pallas_call | solution.py:821
  138.2 1.9 %copy.18 = bf16[128,2048]{1,0:T(8,128)(2,1)} copy(bf16[128,2048]{1,0:T(8,128)(2,1)} %shard_map.154) | data formatting | bytes 1048576

commit v6 on v5

--- a/solution.py
+++ b/solution.py
@@ -25,6 +25,7 @@
 TILE = D // COLUMN
 FLAT = 16
 SENT = STATE + 16
+PAIR = 2 * CAP
 
 EXACT = lax.Precision.HIGHEST
 MESH = pl.DeviceIdType.MESH
@@ -105,9 +106,11 @@
         "lent_y": vmem((4, PICK, D), bf16),
         "back_y": vmem((4, PICK, D), bf16),
         "select": vmem((4, 2 * PICK, WIDE), bf16),
-        "gate_col": vmem((4, 2 * PICK, BLOCK), f32),
+        "weigh": vmem((4, WIDE, 2 * PICK), bf16),
         "part": vmem((16 * BLOCK, D), bf16),
-        "land": vmem((15 * BLOCK, D), bf16),
+        "land": vmem((3 * BLOCK + 4 * (2 * PAIR + BLOCK), D), bf16),
+        "pack": vmem((8, PAIR, D), bf16),
+        "fold": vmem((8, BLOCK, PAIR), bf16),
         "done": vmem((BLOCK, D), bf16),
         "load_sem": dma((16,)),
         "halo_send": dma((1,)),
@@ -118,16 +121,16 @@
         "second_recv": dma((FLAT,)),
         "third_send": dma((COLUMN,)),
         "third_recv": dma((COLUMN,)),
-        "row_send": dma((30,)),
-        "row_recv": dma((30,)),
+        "row_send": dma((22,)),
+        "row_recv": dma((22,)),
         "meta_send": dma((15,)),
         "meta_recv": dma((15,)),
         "lent_send": dma((4,)),
         "lent_recv": dma((4,)),
         "back_send": dma((4,)),
         "back_recv": dma((4,)),
-        "sum_send": dma((30,)),
-        "sum_recv": dma((30,)),
+        "sum_send": dma((18,)),
+        "sum_recv": dma((18,)),
     }
 
 
@@ -139,8 +142,8 @@
     core = ctx % 2
     column = ctx // 2
     me = core * 4 + depth
-    score_rows, finish = mix_rows(r, ctx, depth, core, column, me)
-    spread_rows(r, ctx, depth, core, column, score_rows)
+    finish_rows, score_rows, finish = mix_rows(r, ctx, depth, core, column, me)
+    spread_rows(r, ctx, depth, core, column, finish_rows, score_rows)
     finish()
 
 
@@ -158,6 +161,28 @@
         ((column - initial + FLAT) % FLAT) * 2 + ((me + COLUMN - 1) % COLUMN) // 4,
         (me + COLUMN - 1) % 4,
     )
+
+    barrier = pltpu.get_barrier_semaphore()
+
+    @pl.loop(1, COLUMN)
+    def _(i):
+        pl.semaphore_signal(
+            barrier, inc=1, device_id=member((me + i) % COLUMN), device_id_type=MESH
+        )
+
+    @pl.loop(1, FLAT)
+    def _(i):
+        pl.semaphore_signal(
+            barrier, inc=1, device_id=peer((column + i) % FLAT), device_id_type=MESH
+        )
+
+    @pl.when(me == COLUMN - 1)
+    def _():
+        pl.semaphore_signal(barrier, inc=1, device_id=after, device_id_type=MESH)
+
+    @pl.when(me == 0)
+    def _():
+        pl.semaphore_signal(barrier, inc=1, device_id=ahead, device_id_type=MESH)
 
     def load(i, src, dst):
         copy = pltpu.make_async_copy(src, dst, r.load_sem.at[i])
@@ -182,28 +207,6 @@
     for i, (src, dst) in enumerate(((r.w_gate, r.wg), (r.w_up, r.wu), (r.w_down, r.wd))):
         load(12 + i, src.at[0], dst)
 
-    barrier = pltpu.get_barrier_semaphore()
-
-    @pl.loop(1, COLUMN)
-    def _(i):
-        pl.semaphore_signal(
-            barrier, inc=1, device_id=member((me + i) % COLUMN), device_id_type=MESH
-        )
-
-    @pl.loop(1, FLAT)
-    def _(i):
-        pl.semaphore_signal(
-            barrier, inc=1, device_id=peer((column + i) % FLAT), device_id_type=MESH
-        )
-
-    @pl.when(me == COLUMN - 1)
-    def _():
-        pl.semaphore_signal(barrier, inc=1, device_id=after, device_id_type=MESH)
-
-    @pl.when(me == 0)
-    def _():
-        pl.semaphore_signal(barrier, inc=1, device_id=ahead, device_id_type=MESH)
-
     row_id = lax.broadcasted_iota(jnp.int32, (BLOCK, BLOCK), 0)
     lane_id = lax.broadcasted_iota(jnp.int32, (BLOCK, BLOCK), 1)
     square_id = [lax.broadcasted_iota(jnp.int32, (HEADS, HEADS), axis) for axis in (0, 1)]
@@ -253,7 +256,7 @@
             acc = acc + r.taps_v[j : j + 1, cols] * full[13 + j : 13 + j + count]
         return (acc * sigmoid(acc)).astype(bf16)
 
-    @pl.loop(0, CONV // 128)
+    @pl.loop(0, CONV // 128, unroll=1)
     def _(n):
         cols = pl.ds(pl.multiple_of(n * 128, 128), 128)
         r.mixed[16:, cols] = convolve(r.padded[16:, cols].astype(f32), BLOCK - 16, cols)
@@ -272,9 +275,14 @@
             preferred_element_type=f32,
         )
 
-    @pl.loop(0, COLUMN)
+    @pl.loop(0, COLUMN, unroll=2)
     def _(m):
         r.earlier[m] = weighted(m, 16, BLOCK - 16)
+
+    for k in range(4):
+        for block in (2, 3 - 2 * (k % 2)):
+            low = (4 * k + block) * BLOCK + PAIR
+            r.rows[low : low + BLOCK - PAIR, :] = jnp.zeros((BLOCK - PAIR, D), bf16)
 
     pl.semaphore_wait(barrier, COLUMN + FLAT - 2 + last + initial)
     halo = remote(
@@ -289,7 +297,7 @@
     for copy in load_rest:
         copy.wait()
 
-    @pl.loop(0, COLUMN)
+    @pl.loop(0, COLUMN, unroll=2)
     def _(m):
         cols = pl.ds(pl.multiple_of(m * TILE, TILE), TILE)
         branch = r.gate_v[:, cols].astype(f32)
@@ -298,7 +306,7 @@
     halo.wait_recv()
     keep = (ctx + depth > 0).astype(f32)
 
-    @pl.loop(0, CONV // 128)
+    @pl.loop(0, CONV // 128, unroll=1)
     def _(n):
         cols = pl.ds(pl.multiple_of(n * 128, 128), 128)
         full = jnp.concatenate(
@@ -318,7 +326,7 @@
         q = i // 2
         return ((core + i) % 2) * 4 + (depth + q + q // 2 - 2 * (q // 3)) % 4
 
-    @pl.loop(0, COLUMN)
+    @pl.loop(0, COLUMN, unroll=2)
     def _(i):
         m = around(COLUMN - 1 - i)
         r.piece[m, 0:STATE, :] = (r.earlier[m] + weighted(m, 0, 16)).astype(bf16)
@@ -357,11 +365,11 @@
             jnp.concatenate(highs, axis=1), diagonal, preferred_element_type=f32
         ) + jnp.dot(jnp.concatenate(lows, axis=1), diagonal, preferred_element_type=f32)
 
-    @pl.loop(0, COLUMN)
+    @pl.loop(0, COLUMN // 2, unroll=2)
     def _(m):
         inside(m)
 
-    @pl.loop(0, COLUMN)
+    @pl.loop(0, COLUMN, unroll=2)
     def _(m):
         @pl.when(m != me)
         def _():
@@ -401,6 +409,18 @@
         def _():
             second_copy(o).start()
 
+    @pl.loop(COLUMN // 2, COLUMN, unroll=2)
+    def _(m):
+        inside(m)
+
+    @pl.loop(0, COLUMN, unroll=2)
+    def _(m):
+        cols = pl.ds(pl.multiple_of(m * TILE, TILE), TILE)
+        weight = jnp.dot(r.entry_cols[...], spread(m, 2, HEAD_DIM, TILE), preferred_element_type=f32)
+        branch = r.branch[:, cols]
+        r.value[:, cols] = r.value[:, cols] * branch
+        r.branch[:, cols] = weight * branch
+
     r.before[...] = jnp.zeros((STATE, TILE), f32)
 
     @pl.loop(1, FLAT)
@@ -420,7 +440,7 @@
             r.third.at[m], r.state.at[slot], r.third_send.at[m], r.third_recv.at[slot], member(m)
         )
 
-    @pl.loop(0, COLUMN)
+    @pl.loop(0, COLUMN, unroll=2)
     def _(i):
         m = around(COLUMN - 1 - i)
         r.third[m] = (r.before[...] * jnp.exp(r.earlier_log[m, 0:1, :]) + r.earlier[m]).astype(bf16)
@@ -443,32 +463,35 @@
 
         cols = pl.ds(pl.multiple_of(m * TILE, TILE), TILE)
         carried = jnp.dot(out_map, r.state[m], preferred_element_type=f32)
-        weight = jnp.dot(r.entry_cols[...], spread(m, 2, HEAD_DIM, TILE), preferred_element_type=f32)
-        v = (r.value[:, cols] + carried * weight) * r.branch[:, cols]
+        v = r.value[:, cols] + carried * r.branch[:, cols]
         r.value[:, cols] = v
         return square + fold(v * v)
 
     zero = jnp.zeros((BLOCK, 128), f32)
-    square = lax.fori_loop(0, COLUMN, carry, zero)
+    square = lax.fori_loop(0, COLUMN, carry, zero, unroll=2)
     scale = lax.rsqrt(jnp.sum(square, axis=1, keepdims=True) * (1.0 / D) + 1e-05)
 
-    def join(m, square):
-        cols = pl.ds(pl.multiple_of(m * TILE, TILE), TILE)
-        out = r.value[:, cols] * scale * r.mixer_gain_v[:, cols]
-        kept = (r.residual_v[:, cols].astype(f32) + out).astype(bf16)
-        r.hidden[:, cols] = kept
-        wide = kept.astype(f32)
-        return square + fold(wide * wide)
-
-    square = lax.fori_loop(0, COLUMN, join, zero)
-    again = lax.rsqrt(jnp.sum(square, axis=1, keepdims=True) * (1.0 / D) + 1e-05)
-
-    @pl.loop(0, COLUMN)
-    def _(m):
-        cols = pl.ds(pl.multiple_of(m * TILE, TILE), TILE)
-        r.rows[0:BLOCK, cols] = (
-            r.hidden[:, cols].astype(f32) * again * r.expert_norm_v[:, cols]
-        ).astype(bf16)
+    def finish_rows(half):
+        span = pl.ds(half * HALF, HALF)
+        mine = scale[half * HALF : (half + 1) * HALF]
+
+        def join(m, square):
+            cols = pl.ds(pl.multiple_of(m * TILE, TILE), TILE)
+            out = r.value[span, cols] * mine * r.mixer_gain_v[:, cols]
+            kept = (r.residual_v[span, cols].astype(f32) + out).astype(bf16)
+            r.hidden[span, cols] = kept
+            wide = kept.astype(f32)
+            return square + fold(wide * wide)
+
+        square = lax.fori_loop(0, COLUMN, join, jnp.zeros((HALF, 128), f32), unroll=2)
+        again = lax.rsqrt(jnp.sum(square, axis=1, keepdims=True) * (1.0 / D) + 1e-05)
+
+        @pl.loop(0, COLUMN, unroll=2)
+        def _(m):
+            cols = pl.ds(pl.multiple_of(m * TILE, TILE), TILE)
+            r.rows[span, cols] = (
+                r.hidden[span, cols].astype(f32) * again * r.expert_norm_v[:, cols]
+            ).astype(bf16)
 
     def score_rows():
         logits = lax.dot_general(
@@ -484,7 +507,7 @@
     def finish():
         halo.wait_send()
 
-        @pl.loop(0, COLUMN)
+        @pl.loop(0, COLUMN, unroll=2)
         def _(m):
             @pl.when(m != me)
             def _():
@@ -497,10 +520,10 @@
             def _():
                 second_copy(o).wait_send()
 
-    return score_rows, finish
-
-
-def spread_rows(r, ctx, depth, core, column, score_rows):
+    return finish_rows, score_rows, finish
+
+
+def spread_rows(r, ctx, depth, core, column, finish_rows, score_rows):
     x = column % 4
     y = column // 4
     sibling = ctx + 1 - 2 * core
@@ -517,20 +540,37 @@
     def ring(stage):
         return (0, 4, 0) if stage == 0 else (4 * (stage - 1), 1, 1)
 
-    def row_copy(stage, kind):
-        base, stride, axis = ring(stage)
-        sem = 6 * stage + kind
-        to = (forth, back)[kind % 2][axis]
+    def sides(k):
+        ahead, behind = (forth[1], back[1]) if k % 2 == 0 else (back[1], forth[1])
+        return ahead, behind, 1 + 2 * (k % 2), 3 - 2 * (k % 2)
+
+    def block_rows(block, low, count):
+        return pl.ds(block * BLOCK + low, count)
+
+    def row_copy(kind):
+        to = (forth, back)[kind % 2][0]
         source, target, low = (
-            (0, 1, 0), (0, 3, HALF), (0, 1, HALF), (0, 3, 0), (1, 2, 0), (3, 2, HALF)
+            (0, 4, 0), (0, 12, HALF), (0, 4, HALF), (0, 12, 0), (4, 8, 0), (12, 8, HALF)
         )[kind]
         return remote(
-            r.rows.at[pl.ds((base + stride * source) * BLOCK + low, HALF)],
-            r.rows.at[pl.ds((base + stride * target) * BLOCK + low, HALF)],
-            r.row_send.at[sem],
-            r.row_recv.at[sem],
+            r.rows.at[block_rows(source, low, HALF)],
+            r.rows.at[block_rows(target, low, HALF)],
+            r.row_send.at[kind],
+            r.row_recv.at[kind],
             to,
         )
+
+    def group_copy(k, kind):
+        ahead, behind, whole, picked = sides(k)
+        sem = 6 + 4 * k + kind
+        if kind < 2:
+            source = r.rows.at[block_rows(4 * k, kind * HALF, HALF)]
+            target, to = block_rows(4 * k + whole, kind * HALF, HALF), ahead
+        elif kind == 2:
+            source, target, to = r.pack.at[k], block_rows(4 * k + picked, 0, PAIR), behind
+        else:
+            source, target, to = r.pack.at[4 + k], block_rows(4 * k + 2, 0, PAIR), ahead
+        return remote(source, r.rows.at[target], r.row_send.at[sem], r.row_recv.at[sem], to)
 
     def meta_copy(stage, kind):
         base, stride, axis = ring(stage)
@@ -544,21 +584,34 @@
             to[axis],
         )
 
-    def sum_copy(stage, kind):
-        base, stride, axis = ring(stage)
-        sem = 6 * stage + kind
-        to = (back, forth)[kind % 2][axis]
+    def sum_copy(kind):
+        to = (back, forth)[kind % 2][0]
         source, low, place = (
-            (2, 0, 0),
-            (2, HALF, HALF),
-            (1, HALF, BLOCK + HALF),
-            (3, 0, 2 * BLOCK),
-            (1, 0, BLOCK),
-            (3, HALF, 2 * BLOCK + HALF),
+            (8, 0, 0),
+            (8, HALF, HALF),
+            (4, HALF, BLOCK + HALF),
+            (12, 0, 2 * BLOCK),
+            (4, 0, BLOCK),
+            (12, HALF, 2 * BLOCK + HALF),
         )[kind]
         return remote(
-            r.part.at[pl.ds((base + stride * source) * BLOCK + low, HALF)],
-            r.land.at[pl.ds(stage * 3 * BLOCK + place, HALF)],
+            r.part.at[block_rows(source, low, HALF)],
+            r.land.at[pl.ds(place, HALF)],
+            r.sum_send.at[kind],
+            r.sum_recv.at[kind],
+            to,
+        )
+
+    def group_land(k, kind):
+        return 3 * BLOCK + k * (2 * PAIR + BLOCK) + kind * PAIR
+
+    def group_sum(k, kind):
+        ahead, behind, whole, picked = sides(k)
+        sem = 6 + 3 * k + kind
+        block, count, to = ((2, PAIR, behind), (picked, PAIR, ahead), (whole, BLOCK, behind))[kind]
+        return remote(
+            r.part.at[block_rows(4 * k + block, 0, count)],
+            r.land.at[pl.ds(group_land(k, kind), count)],
             r.sum_send.at[sem],
             r.sum_recv.at[sem],
             to,
@@ -578,106 +631,117 @@
             r.lent_y.at[k], r.back_y.at[k], r.back_send.at[k], r.back_recv.at[k], across
         )
 
-    def send_rows(stage, *kinds):
-        for kind in kinds:
-            row_copy(stage, kind).start()
-
     def send_meta(stage):
         meta_copy(stage, 0).start()
         meta_copy(stage, 1).start()
-
-    def pass_rows(stage, kind):
-        row_copy(stage, kind).wait_recv()
-        row_copy(stage, kind + 4).start()
-
-    def pass_both(stage):
-        meta_copy(stage, 0).wait_recv()
-        meta_copy(stage, 2).start()
-        pass_rows(stage, 0)
-        pass_rows(stage, 1)
-
-    def arrive(stage):
-        for kind in (1, 2):
-            meta_copy(stage, kind).wait_recv()
-        for kind in (2, 3, 4, 5):
-            row_copy(stage, kind).wait_recv()
 
     before = (
         lax.broadcasted_iota(jnp.int32, (BLOCK, BLOCK), 0)
         < lax.broadcasted_iota(jnp.int32, (BLOCK, BLOCK), 1)
     ).astype(bf16)
     slot_row = lax.broadcasted_iota(jnp.int32, (PICK, WIDE), 0).astype(f32)
+    slot_lane = lax.broadcasted_iota(jnp.int32, (BLOCK, 2 * PICK), 1).astype(f32)
+
+    tall = lax.broadcasted_iota(jnp.int32, (BLOCK, BLOCK), 0).astype(f32)
+
+    def ranks(live):
+        return jnp.dot(live.astype(bf16), before, preferred_element_type=f32)
+
+    def gate_row(block, expert):
+        return r.meta[block, pl.ds(expert, 1), :]
+
+    def wanted(either):
+        live = jnp.broadcast_to(either, (8, BLOCK)) > 0.0
+        return jnp.where(tall == jnp.where(live, ranks(live), -1.0)[0:1], 1.0, 0.0)
+
+    def pack_rows(slot, block, to):
+        expert = (to[0] // 2) * 2
+        pick = wanted(jnp.maximum(gate_row(block, expert), gate_row(block, expert + 1)))
+        r.fold[slot] = pick.T[:, :PAIR].astype(bf16)
+        pick = pick[:PAIR].astype(bf16)
+
+        r.pack[slot] = jnp.dot(
+            pick, r.rows[block_rows(block, 0, BLOCK), :], preferred_element_type=f32
+        ).astype(bf16)
+
+    def send_picked(k):
+        pack_rows(k, 4 * k, sides(k)[1])
+        group_copy(k, 2).start()
+
+    def pass_picked(k):
+        group_copy(k, 0).wait_recv()
+        group_copy(k, 1).wait_recv()
+        pack_rows(4 + k, 4 * k + sides(k)[2], sides(k)[0])
+        group_copy(k, 3).start()
+
+    def compacted(own, other):
+        pick = wanted(jnp.maximum(own, other)).astype(bf16)
+        rest = jnp.concatenate([own, other], axis=0)
+        terms = []
+        for _ in range(3):
+            term = rest.astype(bf16).astype(f32)
+            terms.append(term)
+            rest = rest - term
+        terms = jnp.concatenate(terms + [jnp.zeros((2, BLOCK), f32)], axis=0).astype(bf16)
+        got = lax.dot_general(terms, pick, (((1,), (1,)), ((), ())), preferred_element_type=f32)
+        return (
+            got[0:1] + got[2:3] + got[4:5],
+            got[1:2] + got[3:4] + got[5:6],
+        )
 
     def choose(k):
-        gate = jnp.concatenate(
-            [
-                r.meta[4 * k + j, pl.ds(expert, 1), :]
-                for expert in (ctx, sibling)
-                for j in range(4)
-            ],
-            axis=0,
-        )
+        pairs = []
+        for j in range(4):
+            pair = (gate_row(4 * k + j, ctx), gate_row(4 * k + j, sibling))
+            pairs.append(compacted(*pair) if j in (2, sides(k)[3]) else pair)
+        gate = jnp.concatenate([pair[e] for e in range(2) for pair in pairs], axis=0)
         live = gate > 0.0
-        rank = jnp.dot(live.astype(bf16), before, preferred_element_type=f32)
+        rank = ranks(live)
         shift = (lax.broadcasted_iota(jnp.int32, (8, BLOCK), 0) % 4).astype(f32) * CAP
         slot = jnp.where(live, rank + shift, -1.0)
         for half in range(2):
             lanes = jnp.concatenate([slot[4 * half + j : 4 * half + j + 1] for j in range(4)], axis=1)
-            value = jnp.concatenate([gate[4 * half + j : 4 * half + j + 1] for j in range(4)], axis=1)
-            hit = slot_row == lanes
             span = pl.ds(half * PICK, PICK)
-            r.select[k, span, :] = jnp.where(hit, 1.0, 0.0).astype(bf16)
-            total = jnp.sum(jnp.where(hit, value, 0.0), axis=1, keepdims=True)
-            r.gate_col[k, span, :] = jnp.broadcast_to(total, (PICK, BLOCK))
-
-        @pl.loop(0, 8)
-        def _(n):
-            cols = pl.ds(pl.multiple_of(n * 256, 256), 256)
-            got = jnp.dot(
-                r.select[k], r.rows[pl.ds(k * WIDE, WIDE), cols], preferred_element_type=f32
+            r.select[k, span, :] = jnp.where(slot_row == lanes, 1.0, 0.0).astype(bf16)
+        upright = jnp.concatenate([slot, gate, jnp.zeros((BLOCK - 16, BLOCK), f32)], axis=0).T
+        for j in range(4):
+            own = jnp.where(slot_lane == upright[:, j : j + 1], upright[:, 8 + j : 9 + j], 0.0)
+            other = jnp.where(
+                slot_lane - PICK == upright[:, 4 + j : 5 + j], upright[:, 12 + j : 13 + j], 0.0
+            )
+            r.weigh[k, pl.ds(j * BLOCK, BLOCK), :] = jnp.where(
+                slot_lane < PICK, own, other
             ).astype(bf16)
-            r.picked[k, pl.ds(0, PICK), cols] = got[:PICK]
-            r.lent[k, :, cols] = got[PICK:]
+
+        got = jnp.dot(
+            r.select[k], r.rows[pl.ds(k * WIDE, WIDE), :], preferred_element_type=f32
+        ).astype(bf16)
+        r.picked[k, pl.ds(0, PICK), :] = got[:PICK]
+        r.lent[k] = got[PICK:]
 
         lent_copy(k).start()
 
     def feed(k):
         lent_copy(k).wait_recv()
 
-        @pl.loop(0, 3)
-        def _(f):
-            cols = pl.ds(pl.multiple_of(f * 256, 256), 256)
-            gate = jnp.dot(r.picked[k], r.wg[:, cols], preferred_element_type=f32)
-            up = jnp.dot(r.picked[k], r.wu[:, cols], preferred_element_type=f32)
-            r.activated[:, cols] = (gate * sigmoid(gate) * up).astype(bf16)
+        gate = jnp.dot(r.picked[k], r.wg[...], preferred_element_type=f32)
+        up = jnp.dot(r.picked[k], r.wu[...], preferred_element_type=f32)
+        r.activated[...] = (gate * sigmoid(gate) * up).astype(bf16)
 
     def produce(k):
-        @pl.loop(0, 8)
-        def _(n):
-            cols = pl.ds(pl.multiple_of(n * 256, 256), 256)
-            made = jnp.dot(r.activated[...], r.wd[:, cols], preferred_element_type=f32)
-            scale = r.gate_col[k, pl.ds(0, PICK), :]
-            r.own_y[:, cols] = (
-                made[:PICK] * jnp.concatenate([scale, scale], axis=1)
-            ).astype(bf16)
-            r.lent_y[k, :, cols] = made[PICK:].astype(bf16)
+        made = jnp.dot(r.activated[...], r.wd[...], preferred_element_type=f32)
+        r.own_y[...] = made[:PICK].astype(bf16)
+        r.lent_y[k] = made[PICK:].astype(bf16)
 
         back_copy(k).start()
 
     def combine(k):
         back_copy(k).wait_recv()
 
-        @pl.loop(0, 8)
-        def _(n):
-            cols = pl.ds(pl.multiple_of(n * 256, 256), 256)
-            scale = r.gate_col[k, pl.ds(PICK, PICK), :]
-            other = (
-                r.back_y[k, :, cols].astype(f32) * jnp.concatenate([scale, scale], axis=1)
-            ).astype(bf16)
-            both = jnp.concatenate([r.own_y[:, cols], other], axis=0)
-            r.part[pl.ds(k * WIDE, WIDE), cols] = lax.dot_general(
-                r.select[k], both, (((0,), (0,)), ((), ())), preferred_element_type=f32
-            ).astype(bf16)
+        both = jnp.concatenate([r.own_y[...], r.back_y[k]], axis=0)
+        r.part[pl.ds(k * WIDE, WIDE), :] = jnp.dot(
+            r.weigh[k], both, preferred_element_type=f32
+        ).astype(bf16)
 
     def add_into(block, low, count, places):
         @pl.loop(0, count // 16)
@@ -688,92 +752,146 @@
                 total += r.land[pl.ds(pl.multiple_of(place + i * 16, 16), 16), :].astype(f32)
             r.part[span, :] = total.astype(bf16)
 
-    def sum_first(stage):
-        for kind in range(4):
-            sum_copy(stage, kind).start()
-
-    def sum_second(stage):
-        base, stride, _ = ring(stage)
-        place = stage * 3 * BLOCK
-        sum_copy(stage, 0).wait_recv()
-        add_into(base + stride, 0, HALF, (place,))
-        sum_copy(stage, 4).start()
-        sum_copy(stage, 1).wait_recv()
-        add_into(base + 3 * stride, HALF, HALF, (place + HALF,))
-        sum_copy(stage, 5).start()
-
-    def sum_last(stage):
-        base, _, _ = ring(stage)
-        place = stage * 3 * BLOCK
-        for kind in (2, 3, 4, 5):
-            sum_copy(stage, kind).wait_recv()
-        if stage > 0:
-            add_into(base, 0, BLOCK, (place + BLOCK, place + 2 * BLOCK))
-
-    send_rows(0, 0, 1, 2, 3)
-    send_rows(1, 0, 1, 2, 3)
+    def expand(block, place, slot):
+        span = block_rows(block, 0, BLOCK)
+        more = jnp.dot(
+            r.fold[slot], r.land[pl.ds(place, PAIR), :], preferred_element_type=f32
+        )
+        r.part[span, :] = (r.part[span, :].astype(f32) + more).astype(bf16)
+
+    def sum_whole(k):
+        group_sum(k, 0).wait_recv()
+        expand(4 * k + sides(k)[2], group_land(k, 0), 4 + k)
+        group_sum(k, 2).start()
+
+    def sum_picked(k):
+        group_sum(k, 1).wait_recv()
+        expand(4 * k, group_land(k, 1), k)
+
+    def sum_block(k):
+        group_sum(k, 2).wait_recv()
+        add_into(4 * k, 0, BLOCK, (group_land(k, 2),))
+
+    def sum_pass(side):
+        sum_copy(side).wait_recv()
+        add_into(12 if side else 4, side * HALF, HALF, (side * HALF,))
+        sum_copy(side + 4).start()
+
+    def load_weights():
+        for i, (src, dst) in enumerate(((r.w_gate, r.wg), (r.w_up, r.wu), (r.w_down, r.wd))):
+            pltpu.make_async_copy(src.at[0], dst, r.load_sem.at[12 + i]).wait()
+
+    finish_rows(0)
+    finish_rows(1)
+    row_copy(1).start()
+    group_copy(0, 0).start()
+    row_copy(0).start()
     score_rows()
     send_meta(0)
     send_meta(1)
+    row_copy(3).start()
+    row_copy(2).start()
+    send_picked(0)
     meta_copy(0, 0).wait_recv()
     meta_copy(0, 2).start()
     send_meta(2)
-    pass_rows(0, 0)
-    send_rows(2, 0, 3)
+    row_copy(0).wait_recv()
+    group_copy(1, 0).start()
+    group_copy(0, 1).start()
+    row_copy(2).wait_recv()
+    group_copy(1, 1).start()
+    row_copy(1).wait_recv()
+    row_copy(5).start()
+    row_copy(4).start()
+    meta_copy(1, 0).wait_recv()
+    meta_copy(1, 2).start()
+    pass_picked(0)
     meta_copy(0, 1).wait_recv()
     send_meta(4)
-    pass_rows(0, 1)
-    row_copy(0, 2).wait_recv()
-    send_rows(2, 1, 2)
-    pass_both(1)
-    row_copy(0, 3).wait_recv()
-    send_rows(4, 1, 2, 0, 3)
-    pass_both(2)
+    group_copy(3, 1).start()
+    row_copy(3).wait_recv()
+    group_copy(3, 0).start()
     meta_copy(0, 2).wait_recv()
     send_meta(3)
-    row_copy(0, 4).wait_recv()
-    send_rows(3, 0, 3)
-    row_copy(0, 5).wait_recv()
-    send_rows(3, 1, 2)
-    arrive(1)
+    row_copy(4).wait_recv()
+    group_copy(2, 0).start()
+    send_picked(1)
+    row_copy(5).wait_recv()
+    group_copy(2, 1).start()
+    meta_copy(1, 1).wait_recv()
+    meta_copy(1, 2).wait_recv()
+    group_copy(0, 2).wait_recv()
+    group_copy(0, 3).wait_recv()
     choose(0)
-    for i, (src, dst) in enumerate(((r.w_gate, r.wg), (r.w_up, r.wu), (r.w_down, r.wd))):
-        pltpu.make_async_copy(src.at[0], dst, r.load_sem.at[12 + i]).wait()
-    pass_both(4)
+    meta_copy(2, 0).wait_recv()
+    meta_copy(2, 2).start()
+    meta_copy(2, 1).wait_recv()
+    pass_picked(1)
+    send_picked(3)
+    load_weights()
     feed(0)
     produce(0)
-    arrive(2)
+    meta_copy(4, 0).wait_recv()
+    meta_copy(4, 2).start()
+    meta_copy(4, 1).wait_recv()
+    pass_picked(3)
+    combine(0)
+    group_sum(0, 1).start()
+    group_sum(0, 0).start()
+    meta_copy(2, 2).wait_recv()
+    group_copy(1, 2).wait_recv()
+    group_copy(1, 3).wait_recv()
     choose(1)
-    combine(0)
-    pass_both(3)
-    sum_first(1)
+    send_picked(2)
+    meta_copy(3, 0).wait_recv()
+    meta_copy(3, 2).start()
+    pass_picked(2)
     feed(1)
     produce(1)
-    arrive(4)
+    meta_copy(4, 2).wait_recv()
+    group_copy(3, 2).wait_recv()
+    group_copy(3, 3).wait_recv()
     choose(3)
+    sum_whole(0)
     combine(1)
-    sum_first(2)
     feed(3)
     produce(3)
-    arrive(3)
+    meta_copy(3, 1).wait_recv()
+    meta_copy(3, 2).wait_recv()
+    group_copy(2, 2).wait_recv()
+    group_copy(2, 3).wait_recv()
     choose(2)
+    group_sum(1, 1).start()
+    group_sum(1, 0).start()
     combine(3)
-    sum_first(4)
-    sum_second(2)
+    group_sum(3, 1).start()
     feed(2)
+    group_sum(3, 0).start()
     produce(2)
-    sum_second(4)
     combine(2)
-    sum_first(3)
-    sum_last(2)
-    sum_last(4)
-    sum_second(3)
-    sum_second(1)
-    sum_last(3)
-    sum_first(0)
-    sum_last(1)
-    sum_second(0)
-    sum_last(0)
+    group_sum(2, 0).start()
+    group_sum(2, 1).start()
+    sum_whole(3)
+    sum_block(0)
+    sum_whole(1)
+    sum_picked(1)
+    sum_whole(2)
+    sum_picked(2)
+    sum_picked(3)
+    sum_block(2)
+    sum_copy(0).start()
+    sum_copy(1).start()
+    sum_block(1)
+    sum_block(3)
+    sum_copy(3).start()
+    sum_copy(2).start()
+    sum_pass(0)
+    sum_pass(1)
+    sum_picked(0)
+    sum_copy(2).wait_recv()
+    sum_copy(3).wait_recv()
+    sum_copy(4).wait_recv()
+    sum_copy(5).wait_recv()
 
     @pl.loop(0, BLOCK // 16)
     def _(i):
@@ -785,12 +903,17 @@
 
     store = pltpu.make_async_copy(r.done, r.out, r.load_sem.at[15])
     store.start()
+    for kind in range(6):
+        row_copy(kind).wait_send()
+        sum_copy(kind).wait_send()
     for stage in range(5):
-        for kind in range(6):
-            row_copy(stage, kind).wait_send()
-            sum_copy(stage, kind).wait_send()
         for kind in range(3):
             meta_copy(stage, kind).wait_send()
+    for k in range(4):
+        for kind in range(4):
+            group_copy(k, kind).wait_send()
+        for kind in range(3):
+            group_sum(k, kind).wait_send()
     for k in range(4):
         lent_copy(k).wait_send()
         back_copy(k).wait_send()

time: 140 us -> 126 us (0.900); the launches traced: 140 us -> 124 us
  Pallas kernels: 138 us -> 122 us
    pallas_call x1, Pallas kernels: 138 us -> 122 us  [layer(): pl.pallas_call(layer_kernel, out_shape=jax.ShapeDtypeStruct((BLOCK, D), b...]
where the time goes in v6:
time: 126 us; the launch traced here: 124 us
  Pallas kernels  122 us (97%)
  local copies, waits for them, and re-layouts  1.88 us (1%)
    pallas_call x1, Pallas kernels, layer(): pl.pallas_call(layer_kernel, out_shape=jax.ShapeDtypeStruct((BLOCK, D), b...  122 us

profile of v6, /device:TPU:0, one launch (start us, length us, event | category | flops | bytes accessed | tf_op | source)
XLA Modules:
  0.0 124.3 jit_solution(11315873586865896015)
XLA Ops:
  0.0 122.4 %shard_map.154 = bf16[128,2048]{1,0:T(8,128)(2,1)} custom-call(bf16[128,2176]{1,0:T(8,128)(2,1)} %refs_0_.1, bf16[128,2048]{1,0:T(8,128)(2,1)} %refs_1_.1, f32[32,128]{1,0:T(8,128)} %refs_2_.1, f32[1,32]{1,0:T(1,128)} %bitcast.10, f32[1,32]{1,0:T(1,128)} %bitcast.11, f32[4,2176]{1,0:T(4,128)} %refs_5_.1, f32[2176]{0:T(1024)} %refs_6_.1, f32[32]{0:T(128)} %refs_7_.1, ...), custom_call_target="tpu_custom_call" | custom-call | tf_op jit(solution)/shard_map/pallas_call | solution.py:944
  122.4 1.9 %copy.18 = bf16[128,2048]{1,0:T(8,128)(2,1)} copy(bf16[128,2048]{1,0:T(8,128)(2,1)} %shard_map.154) | data formatting | bytes 1048576

commit v7 on v6

--- a/solution.py
+++ b/solution.py
@@ -782,78 +782,80 @@
             pltpu.make_async_copy(src.at[0], dst, r.load_sem.at[12 + i]).wait()
 
     finish_rows(0)
-    finish_rows(1)
-    row_copy(1).start()
+    row_copy(3).start()
     group_copy(0, 0).start()
     row_copy(0).start()
+    finish_rows(1)
     score_rows()
     send_meta(0)
     send_meta(1)
-    row_copy(3).start()
+    row_copy(1).start()
+    group_copy(0, 1).start()
     row_copy(2).start()
     send_picked(0)
+    meta_copy(0, 1).wait_recv()
+    send_meta(4)
+    row_copy(3).wait_recv()
+    group_copy(3, 0).start()
+    row_copy(0).wait_recv()
+    row_copy(4).start()
     meta_copy(0, 0).wait_recv()
     meta_copy(0, 2).start()
     send_meta(2)
-    row_copy(0).wait_recv()
     group_copy(1, 0).start()
-    group_copy(0, 1).start()
     row_copy(2).wait_recv()
     group_copy(1, 1).start()
-    row_copy(1).wait_recv()
-    row_copy(5).start()
-    row_copy(4).start()
     meta_copy(1, 0).wait_recv()
     meta_copy(1, 2).start()
     pass_picked(0)
-    meta_copy(0, 1).wait_recv()
-    send_meta(4)
+    row_copy(1).wait_recv()
     group_copy(3, 1).start()
-    row_copy(3).wait_recv()
-    group_copy(3, 0).start()
-    meta_copy(0, 2).wait_recv()
-    send_meta(3)
-    row_copy(4).wait_recv()
-    group_copy(2, 0).start()
     send_picked(1)
-    row_copy(5).wait_recv()
-    group_copy(2, 1).start()
+    meta_copy(2, 0).wait_recv()
+    meta_copy(2, 2).start()
+    meta_copy(2, 1).wait_recv()
+    pass_picked(1)
     meta_copy(1, 1).wait_recv()
     meta_copy(1, 2).wait_recv()
     group_copy(0, 2).wait_recv()
     group_copy(0, 3).wait_recv()
     choose(0)
-    meta_copy(2, 0).wait_recv()
-    meta_copy(2, 2).start()
-    meta_copy(2, 1).wait_recv()
-    pass_picked(1)
     send_picked(3)
+    meta_copy(0, 2).wait_recv()
+    send_meta(3)
+    row_copy(4).wait_recv()
+    group_copy(2, 0).start()
+    row_copy(5).start()
     load_weights()
     feed(0)
     produce(0)
+    meta_copy(2, 2).wait_recv()
+    group_copy(1, 2).wait_recv()
+    group_copy(1, 3).wait_recv()
+    choose(1)
     meta_copy(4, 0).wait_recv()
     meta_copy(4, 2).start()
     meta_copy(4, 1).wait_recv()
     pass_picked(3)
+    row_copy(5).wait_recv()
+    group_copy(2, 1).start()
     combine(0)
+    group_sum(0, 0).start()
+    send_picked(2)
     group_sum(0, 1).start()
-    group_sum(0, 0).start()
-    meta_copy(2, 2).wait_recv()
-    group_copy(1, 2).wait_recv()
-    group_copy(1, 3).wait_recv()
-    choose(1)
-    send_picked(2)
+    feed(1)
+    produce(1)
     meta_copy(3, 0).wait_recv()
     meta_copy(3, 2).start()
     pass_picked(2)
-    feed(1)
-    produce(1)
     meta_copy(4, 2).wait_recv()
     group_copy(3, 2).wait_recv()
     group_copy(3, 3).wait_recv()
     choose(3)
+    combine(1)
     sum_whole(0)
-    combine(1)
+    group_sum(1, 1).start()
+    group_sum(1, 0).start()
     feed(3)
     produce(3)
     meta_copy(3, 1).wait_recv()
@@ -861,33 +863,31 @@
     group_copy(2, 2).wait_recv()
     group_copy(2, 3).wait_recv()
     choose(2)
-    group_sum(1, 1).start()
-    group_sum(1, 0).start()
     combine(3)
     group_sum(3, 1).start()
+    group_sum(3, 0).start()
     feed(2)
-    group_sum(3, 0).start()
     produce(2)
     combine(2)
     group_sum(2, 0).start()
     group_sum(2, 1).start()
+    sum_block(0)
     sum_whole(3)
-    sum_block(0)
+    sum_whole(2)
+    sum_picked(1)
+    sum_picked(2)
     sum_whole(1)
-    sum_picked(1)
-    sum_whole(2)
-    sum_picked(2)
-    sum_picked(3)
     sum_block(2)
     sum_copy(0).start()
     sum_copy(1).start()
+    sum_block(3)
+    sum_picked(3)
+    sum_copy(3).start()
     sum_block(1)
-    sum_block(3)
-    sum_copy(3).start()
     sum_copy(2).start()
+    sum_picked(0)
     sum_pass(0)
     sum_pass(1)
-    sum_picked(0)
     sum_copy(2).wait_recv()
     sum_copy(3).wait_recv()
     sum_copy(4).wait_recv()

time: 126 us -> 123 us (0.976)
  Pallas kernels: 122 us -> 120 us
    pallas_call x1, Pallas kernels: 122 us -> 120 us  [layer(): pl.pallas_call(layer_kernel, out_shape=jax.ShapeDtypeStruct((BLOCK, D), b...]
where the time goes in v7:
time: 123 us; the launch traced here: 122 us
  Pallas kernels  120 us (98%)
  local copies, waits for them, and re-layouts  1.88 us (2%)
    pallas_call x1, Pallas kernels, layer(): pl.pallas_call(layer_kernel, out_shape=jax.ShapeDtypeStruct((BLOCK, D), b...  120 us

profile of v7, /device:TPU:0, one launch (start us, length us, event | category | flops | bytes accessed | tf_op | source)
XLA Modules:
  0.0 121.9 jit_solution(14189707465431688018)
XLA Ops:
  0.0 120.0 %shard_map.154 = bf16[128,2048]{1,0:T(8,128)(2,1)} custom-call(bf16[128,2176]{1,0:T(8,128)(2,1)} %refs_0_.1, bf16[128,2048]{1,0:T(8,128)(2,1)} %refs_1_.1, f32[32,128]{1,0:T(8,128)} %refs_2_.1, f32[1,32]{1,0:T(1,128)} %bitcast.10, f32[1,32]{1,0:T(1,128)} %bitcast.11, f32[4,2176]{1,0:T(4,128)} %refs_5_.1, f32[2176]{0:T(1024)} %refs_6_.1, f32[32]{0:T(128)} %refs_7_.1, ...), custom_call_target="tpu_custom_call" | custom-call | tf_op jit(solution)/shard_map/pallas_call | solution.py:944
  120.0 1.9 %copy.18 = bf16[128,2048]{1,0:T(8,128)(2,1)} copy(bf16[128,2048]{1,0:T(8,128)(2,1)} %shard_map.154) | data formatting | bytes 1048576
